TPU v7x, 512 devices: a whole 4x4x16 slice. The times are simulated.
512 devices in a mesh: ctx: 64 (over z_lo, x, core), grp: 8 (over z_hi, y).
Axes of the slice: x: 4, y: 4, z: 16 (z_hi: 2, z_lo: 8; z = z_hi * 8 + z_lo), core: 2. Of those that a mesh axis runs over, the one named last changes fastest.
Arguments:
- q_prompt: bfloat16 [4096, 64, 128], P('ctx', 'grp'), may hold values from -8 to 8
- k_prompt: bfloat16 [4096, 8, 128], P(('ctx', 'grp')), may hold values from -8 to 8
- v_prompt: bfloat16 [4096, 8, 128], P(('ctx', 'grp')), may hold values from -6 to 6
- grad_prompt: bfloat16 [4096, 64, 128], P('ctx', 'grp'), may hold values from -12 to 12
- q_roll: bfloat16 [4096, 64, 128], P('ctx', 'grp'), may hold values from -8 to 8
- k_roll: bfloat16 [4096, 8, 128], P('ctx', 'grp'), may hold values from -6 to 6
- v_roll: bfloat16 [4096, 8, 128], P('ctx', 'grp'), may hold values from -6 to 6
- grad_roll: bfloat16 [4096, 64, 128], P('ctx', 'grp'), may hold values from -12 to 12
- prompt_len: int32 [1], replicated, may hold values from 2049 to 4096
- roll_len: int32 [16], replicated, may hold values from 1 to 256, 3072 in all
Outputs:
- dq_prompt: bfloat16 [4096, 64, 128], P('ctx', 'grp')
- dk_prompt: bfloat16 [4096, 8, 128], P(('ctx', 'grp'))
- dv_prompt: bfloat16 [4096, 8, 128], P(('ctx', 'grp'))
- dq_roll: bfloat16 [4096, 64, 128], P('ctx', 'grp')
- dk_roll: bfloat16 [4096, 8, 128], P('ctx', 'grp')
- dv_roll: bfloat16 [4096, 8, 128], P('ctx', 'grp')
Inputs may be any that keep to these rules, and one draw needn't show every extreme that they name: `roll_len`: some rollout has length 256.
All inputs are finite; a program needn't handle non-finite values.
Results may differ from a plain program's by a relative error of at most 0.0091.
Values may be sent and summed in bfloat16 or wider, within the bound.
No kernel may reach another device: no remote copies, remote signals or barrier semaphores. Data moves between devices by JAX's collectives and lax.ppermute only.
A program may use at most 64 MiB of HBM per device.

v0:
```python
import math

import jax
import jax.numpy as jnp
from jax import lax
from jax.sharding import PartitionSpec as P

RSPLIT = 4


VERY_NEGATIVE = -1e30


def from_behind(value, axis, steps):
    count = lax.axis_size(axis)
    first, last = (max(0, -steps), min(count, count - steps))
    return lax.ppermute(value, axis, [(source, source + steps) for source in range(first, last)])


def block_scores(queries, key_block, visible, scaling):
    scores = (
        jnp.einsum("rkgd,jkd->kgrj", queries, key_block, preferred_element_type=jnp.float32)
        * scaling
    )
    return jnp.where(visible[None, None], scores, -jnp.inf)


def merge_stats(running, queries, key_block, visible, scaling):
    row_max, row_sum = running
    scores = block_scores(queries, key_block, visible, scaling)
    new_max = jnp.maximum(row_max, jnp.max(scores, axis=-1))
    row_sum = row_sum * jnp.exp(row_max - new_max) + jnp.sum(
        jnp.exp(scores - new_max[..., None]), axis=-1
    )
    return (new_max, row_sum)


def block_output(queries, key_block, value_block, visible, log_total, scaling):
    weights = jnp.exp(block_scores(queries, key_block, visible, scaling) - log_total[..., None])
    rounded = weights.astype(jnp.bfloat16)
    return jnp.einsum("kgrj,jkd->rkgd", rounded, value_block, preferred_element_type=jnp.float32)


def block_grads(
    queries, out_grads, key_block, value_block, visible, log_total, delta_term, scaling
):
    weights = jnp.exp(block_scores(queries, key_block, visible, scaling) - log_total[..., None])
    rounded = weights.astype(jnp.bfloat16)
    weight_grad = jnp.einsum(
        "rkgd,jkd->kgrj", out_grads, value_block, preferred_element_type=jnp.float32
    )
    score_grad = (weights * (weight_grad - delta_term[..., None])).astype(jnp.bfloat16)
    query_part = jnp.einsum(
        "kgrj,jkd->rkgd", score_grad, key_block, preferred_element_type=jnp.float32
    )
    key_part = (
        jnp.einsum("kgrj,rkgd->jkd", score_grad, queries, preferred_element_type=jnp.float32)
        * scaling
    )
    value_part = jnp.einsum(
        "kgrj,rkgd->jkd", rounded, out_grads, preferred_element_type=jnp.float32
    )
    return (query_part, jnp.concatenate([key_part, value_part], axis=-1))


def per_device(
    q_prompt,
    k_prompt,
    v_prompt,
    grad_prompt,
    q_roll,
    k_roll,
    v_roll,
    grad_roll,
    prompt_len,
    roll_len,
):
    kv_local = k_roll.shape[1]
    head_dim = q_prompt.shape[2]
    heads_local = q_prompt.shape[1]
    per_group = heads_local // kv_local
    prompt_rows = q_prompt.shape[0]
    roll_rows = q_roll.shape[0]
    row_count = prompt_rows + roll_rows
    ctx_size = lax.axis_size("ctx")
    prompt_total = prompt_rows * ctx_size
    scaling = 1.0 / math.sqrt(head_dim)
    own_heads = (
        lax.all_to_all(k_prompt, "grp", split_axis=1, concat_axis=0, tiled=True),
        lax.all_to_all(v_prompt, "grp", split_axis=1, concat_axis=0, tiled=True),
    )
    keys_all, values_all = (
        lax.all_gather(own_heads[0], "ctx", axis=0, tiled=True),
        lax.all_gather(own_heads[1], "ctx", axis=0, tiled=True),
    )
    ctx_index = lax.axis_index("ctx")
    roll_block = ctx_index % RSPLIT
    prompt_limit = prompt_len[0]
    roll_limit = lax.dynamic_index_in_dim(roll_len, ctx_index // RSPLIT, 0, keepdims=False)
    prompt_pos = ctx_index * prompt_rows + jnp.arange(prompt_rows, dtype=jnp.int32)
    roll_pos = roll_block * roll_rows + jnp.arange(roll_rows, dtype=jnp.int32)
    row_valid = jnp.concatenate([prompt_pos < prompt_limit, roll_pos < roll_limit])
    queries = jnp.concatenate([q_prompt, q_roll], axis=0).reshape(
        row_count, kv_local, per_group, head_dim
    )
    out_grads = (
        jnp.concatenate([grad_prompt, grad_roll], axis=0)
        * row_valid.astype(jnp.bfloat16)[:, None, None]
    )
    out_grads = out_grads.reshape(row_count, kv_local, per_group, head_dim)
    prompt_cap = jnp.concatenate([prompt_pos, jnp.full((roll_rows,), prompt_total, jnp.int32)])
    roll_cap = jnp.concatenate([jnp.full((prompt_rows,), -1, jnp.int32), roll_pos])
    own_pair = jnp.concatenate([k_roll, v_roll], axis=-1)
    pair_list = [own_pair]
    position_list = [roll_pos]
    usable_list = [jnp.ones((roll_rows,), bool)]
    for distance in range(1, RSPLIT):
        arrived = from_behind(own_pair, "ctx", distance)
        pair_list.append(arrived)
        position_list.append(roll_pos - distance * roll_rows)
        usable_list.append(jnp.broadcast_to(roll_block >= distance, (roll_rows,)))
    roll_pairs = jnp.concatenate(pair_list, axis=0)
    roll_keys = roll_pairs[..., :head_dim]
    roll_values = roll_pairs[..., head_dim:]
    roll_key_pos = jnp.concatenate(position_list)
    roll_key_usable = jnp.concatenate(usable_list)
    roll_seen = roll_key_usable[None, :] & (roll_key_pos[None, :] <= roll_cap[:, None])
    key_width = math.gcd(prompt_total, 512)
    key_blocks = prompt_total // key_width

    def prompt_block(first_row, row_total):
        key_block = lax.dynamic_slice_in_dim(keys_all, first_row, row_total, 0)
        value_block = lax.dynamic_slice_in_dim(values_all, first_row, row_total, 0)
        key_pos = first_row + jnp.arange(row_total, dtype=jnp.int32)
        visible = (key_pos[None, :] < prompt_limit) & (key_pos[None, :] <= prompt_cap[:, None])
        return (key_block, value_block, visible)

    def stats_step(step, running):
        key_block, value_block, visible = prompt_block(step * key_width, key_width)
        return merge_stats(running, queries, key_block, visible, scaling)

    start_stats = (
        jnp.full((kv_local, per_group, row_count), VERY_NEGATIVE, jnp.float32),
        jnp.zeros((kv_local, per_group, row_count), jnp.float32),
    )
    running = lax.fori_loop(0, key_blocks, stats_step, start_stats)
    row_max, row_sum = merge_stats(running, queries, roll_keys, roll_seen, scaling)
    log_total = row_max + jnp.log(row_sum)

    def output_step(step, attended):
        key_block, value_block, visible = prompt_block(step * key_width, key_width)
        return attended + block_output(queries, key_block, value_block, visible, log_total, scaling)

    attended = lax.fori_loop(
        0,
        key_blocks,
        output_step,
        block_output(queries, roll_keys, roll_values, roll_seen, log_total, scaling),
    )
    delta_term = jnp.transpose(
        jnp.sum(out_grads.astype(jnp.float32) * attended, axis=-1), (1, 2, 0)
    )
    roll_query_part, roll_kv = block_grads(
        queries, out_grads, roll_keys, roll_values, roll_seen, log_total, delta_term, scaling
    )
    roll_total = roll_kv[:roll_rows]
    for distance in range(1, RSPLIT):
        returned_part = from_behind(
            roll_kv[distance * roll_rows : (distance + 1) * roll_rows], "ctx", -distance
        )
        same_rollout = (roll_block + distance < RSPLIT).astype(jnp.float32)
        roll_total = roll_total + returned_part * same_rollout

    def grad_step(step, state):
        query_acc, partial_value = state
        key_block, value_block, visible = prompt_block(step * key_width, key_width)
        query_part, kv_part = block_grads(
            queries, out_grads, key_block, value_block, visible, log_total, delta_term, scaling
        )
        return (
            query_acc + query_part,
            lax.dynamic_update_slice_in_dim(partial_value, kv_part, step * key_width, 0),
        )

    empty_terms = jnp.zeros((prompt_total, kv_local, 2 * head_dim), jnp.float32)
    query_acc, partial_value = lax.fori_loop(
        0, key_blocks, grad_step, (roll_query_part, empty_terms)
    )
    summed = lax.psum_scatter(partial_value, "ctx", scatter_dimension=0, tiled=True)
    query_out = (query_acc * scaling).astype(jnp.bfloat16).reshape(row_count, heads_local, head_dim)
    dq_prompt = query_out[:prompt_rows]
    dq_roll = query_out[prompt_rows:]
    roll_out = roll_total.astype(jnp.bfloat16)
    dk_roll = roll_out[..., :head_dim]
    dv_roll = roll_out[..., head_dim:]
    returned = lax.all_to_all(
        summed.astype(jnp.bfloat16), "grp", split_axis=0, concat_axis=1, tiled=True
    )
    dk_prompt = returned[..., :head_dim]
    dv_prompt = returned[..., head_dim:]
    return (dq_prompt, dk_prompt, dv_prompt, dq_roll, dk_roll, dv_roll)


def solution(mesh):
    return jax.shard_map(
        per_device,
        mesh=mesh,
        in_specs=(
            P("ctx", "grp", None),
            P(("ctx", "grp"), None, None),
            P(("ctx", "grp"), None, None),
            P("ctx", "grp", None),
            P("ctx", "grp", None),
            P("ctx", "grp", None),
            P("ctx", "grp", None),
            P("ctx", "grp", None),
            P(),
            P(),
        ),
        out_specs=(
            P("ctx", "grp", None),
            P(("ctx", "grp"), None, None),
            P(("ctx", "grp"), None, None),
            P("ctx", "grp", None),
            P("ctx", "grp", None),
            P("ctx", "grp", None),
        ),
        check_vma=False,
    )
```

profile of v0, /device:TPU:8, one launch (start us, length us, event | category | flops | bytes accessed | tf_op | source)
XLA Modules:
  0.0 957.0 jit_solution(12259701966924405163)
XLA Ops:
  8.5 18.2 %all-to-all-start = ((bf16[8,8,128]{2,0,1:T(8,128)(2,1)}), bf16[8,8,128]{2,0,1:T(8,128)(2,1)S(1)}, u32[]{:S(2)}, u32[]{:S(2)}) async-start(bf16[8,8,128]{2,0,1:T(8,128)(2,1)} %copy.111), calls=%async_computation | async-start | bytes 32768 | tf_op jit(solution)/shard_map/all_to_all | solution.py:89
  28.1 2.3 collective-permute-start.2
  30.4 3.4 collective-permute-start.1
  33.8 3.5 collective-permute-start
  40.1 13.6 %all-to-all-start.1 = ((bf16[8,8,128]{2,0,1:T(8,128)(2,1)}), bf16[8,8,128]{2,0,1:T(8,128)(2,1)S(1)}, u32[]{:S(2)}, u32[]{:S(2)}) async-start(bf16[8,8,128]{2,0,1:T(8,128)(2,1)} %copy.117), calls=%async_computation.1 | async-start | bytes 32768 | tf_op jit(solution)/shard_map/all_to_all | solution.py:90
  60.0 1.8 copy.113
  61.7 1.8 copy.114
  67.8 109.4 %all-gather.3.cloned.1.call-done = bf16[4096,1,128]{2,0,1:T(8,128)(2,1)} async-done(((bf16[64,1,128]{2,0,1:T(8,128)(2,1)}), bf16[4096,1,128]{2,0,1:T(8,128)(2,1)}) %all-gather.3.cloned.1.call-update) | async-done | bytes 1048592 | tf_op jit(solution)/shard_map/all_gather | solution.py:93
  177.3 22.0 %while.46 = (s32[]{:T(128)}, f32[1,8,128]{2,1,0:T(8,128)S(1)}, f32[1,8,128]{2,1,0:T(8,128)S(1)}, s32[]{:T(128)}, s32[128]{0:T(128)S(1)}, /*index=5*/bf16[4096,1,...) while((s32[]{:T(128)}, f32[1,8,128]{2,1,0:T(8,128)S(1)}, ...), condition=%wide.region_3.4_spmd.clone, body=%wide.region_0.3_spmd.clone.sunk | while | flops 138025472 | bytes 4843198 | solution.py:146
  200.3 94.7 %all-gather.5.cloned.1.call-done = bf16[4096,1,128]{2,0,1:T(8,128)(2,1)} async-done(((bf16[64,1,128]{2,0,1:T(8,128)(2,1)}), bf16[4096,1,128]{2,0,1:T(8,128)(2,1)}) %all-gather.5.cloned.1.call-update) | async-done | bytes 1048592 | tf_op jit(solution)/shard_map/all_gather | solution.py:94
  295.0 21.5 %while.44 = (s32[]{:T(128)}, f32[128,1,8,128]{0,3,2,1:T(8,128)S(1)}, bf16[4096,1,128]{2,0,1:T(8,128)(2,1)}, s32[]{:T(128)}, s32[128]{0:T(128)S(1)}, /*index=5*/b...) while((s32[]{:T(128)}, ...), condition=%wide.region_7.8_spmd, body=%wide.region_6.7_spmd.sunk | while | flops 270796288 | bytes 1714863 | solution.py:154
  295.9 1.8 fusion.105
  298.6 1.8 fusion.105
  301.3 1.8 fusion.105
  304.0 1.8 fusion.105
  306.7 1.8 fusion.105
  309.3 1.8 fusion.105
  312.0 1.8 fusion.105
  314.7 1.8 fusion.105
  322.9 4.6 broadcast_in_dim.168.clone
  327.5 60.2 %while.45 = (s32[]{:T(128)}, f32[128,1,8,128]{0,3,2,1:T(8,128)S(1)}, f32[4096,1,256]{2,1,0:T(1,128)}, bf16[4096,1,128]{2,0,1:T(8,128)(2,1)}, s32[]{:T(128)}, /*i...) while((s32[]{:T(128)}, ...), condition=%wide.region_10.11_spmd, body=%wide.region_9.10_spmd.sunk | while | flops 675218944 | bytes 15742679 | solution.py:186
  328.4 1.5 fusion.116
  335.9 1.5 fusion.116
  343.4 1.5 fusion.116
  350.9 1.5 fusion.116
  358.5 1.5 fusion.116
  366.0 1.5 fusion.116
  373.5 1.5 fusion.116
  381.1 1.5 fusion.116
  387.7 534.9 %all-reduce.4 = bf16[4096,1,256]{2,1,0:T(2,128)(2,1)} all-reduce(f32[4096,1,256]{2,1,0:T(1,128)} %get-tuple-element.459), channel_id=2, replica_groups=mesh['ctx'=64,'grp'=8] {'ctx'}, use_global_device_ids=true, to_apply=%region_11.12.clone | all-reduce | flops 1048576 | bytes 6291456
  925.4 9.9 %all-to-all-start.2 = ((bf16[8,2,1024]{2,1,0:T(2,128)(2,1)}), bf16[8,2,1024]{2,1,0:T(2,128)(2,1)S(1)}, u32[]{:S(2)}, u32[]{:S(2)}) async-start(bf16[8,2,1024]{2,1,0:T(2,128)(2,1)} %reshape.493), calls=%async_computation.2 | async-start | bytes 65536 | tf_op jit(solution)/shard_map/all_to_all | solution.py:196
  937.8 11.0 %all-to-all-done.2 = bf16[8,2,1024]{2,1,0:T(2,128)(2,1)S(1)} async-done(((bf16[8,2,1024]{2,1,0:T(2,128)(2,1)}), bf16[8,2,1024]{2,1,0:T(2,128)(2,1)S(1)}, u32[]{:S(2)}, u32[]{:S(2)}) %all-to-all-start.2) | async-done | bytes 32800 | tf_op jit(solution)/shard_map/all_to_all | solution.py:196
  (245 shorter events, 104.9 us)
Async XLA Ops:
  8.5 31.6 %all-to-all-start = ((bf16[8,8,128]{2,0,1:T(8,128)(2,1)}), bf16[8,8,128]{2,0,1:T(8,128)(2,1)S(1)}, u32[]{:S(2)}, u32[]{:S(2)}) async-start(bf16[8,8,128]{2,0,1:T(8,128)(2,1)} %copy.111), calls=%async_computation | async-start | bytes 32768 | tf_op jit(solution)/shard_map/all_to_all | solution.py:89
  28.1 37.5 %collective-permute-start.2 = (bf16[64,1,256]{2,0,1:T(8,128)(2,1)S(1)}, bf16[64,1,256]{2,0,1:T(8,128)(2,1)S(1)}, u32[]{:S(2)}, u32[]{:S(2)}) collective-permute-start(bf16[64,1,256]{2,0,1:T(8,128)(2,1)S(1)} %constant_dynamic-update-slice_fusion.1), channel_id=1, source_target_pairs={{0,24},{8,32},{16,40},{24,48},{32,56},{40,64},{48,72},{56,80},{64,... | collective-permute-start | bytes 98312 | tf_op jit(solution)/shard_map/ppermute | solution.py:17
  30.4 35.3 %collective-permute-start.1 = (bf16[64,1,256]{2,0,1:T(8,128)(2,1)S(1)}, bf16[64,1,256]{2,0,1:T(8,128)(2,1)S(1)}, u32[]{:S(2)}, u32[]{:S(2)}) collective-permute-start(bf16[64,1,256]{2,0,1:T(8,128)(2,1)S(1)} %constant_dynamic-update-slice_fusion.1), channel_id=1, source_target_pairs={{0,16},{8,24},{16,32},{24,40},{32,48},{40,56},{48,64},{56,72},{64,... | collective-permute-start | bytes 98312 | tf_op jit(solution)/shard_map/ppermute | solution.py:17
  33.8 31.9 %collective-permute-start = (bf16[64,1,256]{2,0,1:T(8,128)(2,1)S(1)}, bf16[64,1,256]{2,0,1:T(8,128)(2,1)S(1)}, u32[]{:S(2)}, u32[]{:S(2)}) collective-permute-start(bf16[64,1,256]{2,0,1:T(8,128)(2,1)S(1)} %constant_dynamic-update-slice_fusion.1), channel_id=1, source_target_pairs={{0,8},{8,16},{16,24},{24,32},{32,40},{40,48},{48,56},{56,64},{64,7... | collective-permute-start | bytes 98312 | tf_op jit(solution)/shard_map/ppermute | solution.py:17
  40.1 13.6 %copy-start.2 = (bf16[8,8,128]{2,0,1:T(8,128)(2,1)}, bf16[8,8,128]{2,0,1:T(8,128)(2,1)S(1)}, u32[]{:S(2)}) copy-start(bf16[8,8,128]{2,0,1:T(8,128)(2,1)S(1)} %all-to-all-done) | copy-start | bytes 49156
  40.1 27.1 %all-to-all-start.1 = ((bf16[8,8,128]{2,0,1:T(8,128)(2,1)}), bf16[8,8,128]{2,0,1:T(8,128)(2,1)S(1)}, u32[]{:S(2)}, u32[]{:S(2)}) async-start(bf16[8,8,128]{2,0,1:T(8,128)(2,1)} %copy.117), calls=%async_computation.1 | async-start | bytes 32768 | tf_op jit(solution)/shard_map/all_to_all | solution.py:90
  53.7 123.6 %all-gather.3.cloned.1.call-start = ((), (), s32[]{:S(2)}) async-start(), calls=%async_computation.3 | async-start | bytes 1064960 | tf_op jit(solution)/shard_map/all_gather | solution.py:93
  54.4 240.5 %all-gather.5.cloned.1.call-start = ((), (), s32[]{:S(2)}) async-start(), calls=%async_computation.4 | async-start | bytes 1064960 | tf_op jit(solution)/shard_map/all_gather | solution.py:94
  67.2 0.6 copy-start.1
  295.0 21.5 %copy-start = (bf16[64,8,128]{0,2,1:T(8,128)(2,1)S(1)}, bf16[64,8,128]{0,2,1:T(8,128)(2,1)}, u32[]{:S(2)}) copy-start(bf16[64,8,128]{0,2,1:T(8,128)(2,1)} %copy.113) | copy-start | bytes 393220
  319.0 617.3 %collective-permute-start.3 = (f32[64,1,256]{0,2,1:T(8,128)S(1)}, f32[64,1,256]{0,2,1:T(8,128)S(1)}, u32[]{:S(2)}, u32[]{:S(2)}) collective-permute-start(f32[64,1,256]{0,2,1:T(8,128)S(1)} %get-tuple-element.640), channel_id=1, source_target_pairs={{8,0},{16,8},{24,16},{32,24},{40,32},{48,40},{56,48},{64,56},{72,6... | collective-permute-start | bytes 196616 | tf_op jit(solution)/shard_map/ppermute | solution.py:17
  320.3 616.0 %collective-permute-start.5 = (f32[64,1,256]{0,2,1:T(8,128)S(1)}, f32[64,1,256]{0,2,1:T(8,128)S(1)}, u32[]{:S(2)}, u32[]{:S(2)}) collective-permute-start(f32[64,1,256]{0,2,1:T(8,128)S(1)} %get-tuple-element.641), channel_id=1, source_target_pairs={{24,0},{32,8},{40,16},{48,24},{56,32},{64,40},{72,48},{80,56},{88,... | collective-permute-start | bytes 196616 | tf_op jit(solution)/shard_map/ppermute | solution.py:17
  321.6 614.7 %collective-permute-start.4 = (f32[64,1,256]{0,2,1:T(8,128)S(1)}, f32[64,1,256]{0,2,1:T(8,128)S(1)}, u32[]{:S(2)}, u32[]{:S(2)}) collective-permute-start(f32[64,1,256]{0,2,1:T(8,128)S(1)} %get-tuple-element.642), channel_id=1, source_target_pairs={{16,0},{24,8},{32,16},{40,24},{48,32},{56,40},{64,48},{72,56},{80,... | collective-permute-start | bytes 196616 | tf_op jit(solution)/shard_map/ppermute | solution.py:17
  925.4 23.4 %all-to-all-start.2 = ((bf16[8,2,1024]{2,1,0:T(2,128)(2,1)}), bf16[8,2,1024]{2,1,0:T(2,128)(2,1)S(1)}, u32[]{:S(2)}, u32[]{:S(2)}) async-start(bf16[8,2,1024]{2,1,0:T(2,128)(2,1)} %reshape.493), calls=%async_computation.2 | async-start | bytes 65536 | tf_op jit(solution)/shard_map/all_to_all | solution.py:196
Sparse Core Ops, SparseCore 0:
  57.3 119.9 all-gather.2
  180.0 114.9 all-gather.4
where the time goes:
time: 959 us; the launch traced here: 957 us
  blocking collectives  535 us (56%)
  waiting for transfers between devices  218 us (23%)
  matrix products  66.8 us (7%)
  starting transfers between devices  54.7 us (6%)
  local copies, waits for them, and re-layouts  36.1 us (4%)
  other arithmetic  29.4 us (3%)
  between operations  15.7 us (2%)
    unnamed x1, blocking collectives  535 us
    all_gather x1, waiting for transfers between devices, per_device(): lax.all_gather(own_heads[0], 'ctx', axis=0, tiled=True)  109 us
    all_gather x1, waiting for transfers between devices, per_device(): lax.all_gather(own_heads[1], 'ctx', axis=0, tiled=True)  94.7 us
    dot_general x17, matrix products, block_scores(): jnp.einsum('rkgd,jkd->kgrj', queries, key_block, preferred_element_type=j...  22.8 us
  transfers between devices with their start and end apart: 11, of which 5 were waited for; matrix products, arithmetic and copies ran while one was open for 11% of the time, Pallas kernels for 0%

commit v1 on v0

v1 whole, which is shorter than its diff:
```python
import functools
import math

import jax
import jax.numpy as jnp
from jax import lax
from jax.experimental import pallas as pl
from jax.experimental.pallas import tpu as pltpu
from jax.sharding import Mesh, PartitionSpec as P

AXES = (("zl", 8), ("x", 4), ("core", 2), ("zh", 2), ("y", 4))
CTX = ("zl", "x", "core")
GRP = ("zh", "y")
FAR = ("zl", "zh", "y")
NEAR = ("x", "core")
X, CORES, ZL = 4, 2, 8
BLOCKS = X * CORES

HD = 128
TOKENS = 64
ROWS = 512
KEYS = ZL * TOKENS
MASKED = -1e30
SCALING = 1.0 / math.sqrt(HD)
LOG2E = math.log2(math.e)
SCALE2 = SCALING * LOG2E
F32 = jnp.float32
BF16 = jnp.bfloat16
NT = (((1,), (1,)), ((), ()))


def shifted(value, axis, steps):
    count = lax.axis_size(axis)
    return lax.ppermute(value, axis, [(i, (i + steps) % count) for i in range(count)])


def place(step, info):
    block, kind = step // 2, step % 2
    owner_x = (info[0] + X - block % X) % X
    owner_core = (info[1] + block // X) % CORES
    return owner_x, owner_core, kind


def stats_index(step, info):
    owner_x, owner_core, kind = place(step, info)
    return (owner_x * CORES + owner_core) * 2 + kind


def load_rows(step, rows_refs, q_s, g_s):
    block = step // 2
    for i in range(BLOCKS):

        @pl.when(block == i)
        def _():
            q_s[...] = rows_refs[2 * i][0]
            g_s[...] = rows_refs[2 * i + 1][0]


def prompt_scores(step, info, keys, queries):
    owner_x, owner_core, kind = place(step, info)
    scores = lax.dot_general(keys, queries, NT, preferred_element_type=F32) * SCALE2
    key = lax.broadcasted_iota(jnp.int32, (KEYS, 1), 0)
    key_pos = (key // TOKENS) * (BLOCKS * TOKENS) + key % TOKENS + (info[0] * CORES + info[1]) * TOKENS
    row = lax.broadcasted_iota(jnp.int32, (1, ROWS), 1)
    first = ((info[2] * X + owner_x) * CORES + owner_core) * TOKENS
    limit = jnp.where(kind == 1, info[3] - 1, first + row // 8)
    return jnp.where(key_pos <= limit, scores, MASKED)


def roll_scores(step, info, keys, queries):
    owner_x, owner_core, _ = place(step, info)
    scores = lax.dot_general(keys, queries, NT, preferred_element_type=F32) * SCALE2
    key_pos = lax.broadcasted_iota(jnp.int32, (TOKENS, 1), 0) + (info[0] * CORES + info[1]) * TOKENS
    row = lax.broadcasted_iota(jnp.int32, (1, ROWS), 1)
    limit = (owner_x * CORES + owner_core) * TOKENS + row // 8
    return jnp.where(key_pos <= limit, scores, MASKED)


def sees_roll(step, info):
    owner_x, _, kind = place(step, info)
    return (kind == 1) & (owner_x // 2 == info[0] // 2)


def partial_stats(scores, weight_grad):
    top = jnp.max(scores, axis=0, keepdims=True)
    weights = jnp.exp2(scores - top)
    total = jnp.sum(weights, axis=0, keepdims=True)
    product = jnp.sum(weights * weight_grad, axis=0, keepdims=True)
    return top + jnp.log2(total), product / total


def merged(first, second):
    (log_a, delta_a), (log_b, delta_b) = first, second
    top = jnp.maximum(log_a, log_b)
    share_a, share_b = jnp.exp2(log_a - top), jnp.exp2(log_b - top)
    total = share_a + share_b
    return top + jnp.log2(total), (delta_a * share_a + delta_b * share_b) / total


def stats_kernel(info, *refs):
    rows_refs, (kv_ref, rkv_ref, stats_ref, q_s, g_s) = refs[: 4 * BLOCKS // 2], refs[4 * BLOCKS // 2 :]
    step = pl.program_id(0)
    load_rows(step, rows_refs, q_s, g_s)
    queries, grads = q_s[...], g_s[...]
    scores = prompt_scores(step, info, kv_ref[:, :HD], queries)
    weight_grad = lax.dot_general(kv_ref[:, HD:], grads, NT, preferred_element_type=F32)
    stats = partial_stats(scores, weight_grad)
    stats_ref[0, 0:1, :] = stats[0]
    stats_ref[0, 1:2, :] = stats[1]

    @pl.when(sees_roll(step, info))
    def _():
        roll = roll_scores(step, info, rkv_ref[:, :HD], queries)
        roll_grad = lax.dot_general(rkv_ref[:, HD:], grads, NT, preferred_element_type=F32)
        both = merged(stats, partial_stats(roll, roll_grad))
        stats_ref[0, 0:1, :] = both[0]
        stats_ref[0, 1:2, :] = both[1]


def block_grads(scores, weight_grad, log_total, delta, queries, grads, keys_t):
    weights = jnp.exp2(scores - log_total)
    rounded = weights.astype(BF16)
    score_grad = (weights * (weight_grad - delta)).astype(BF16)
    key_part = jnp.dot(score_grad, queries, preferred_element_type=F32) * SCALING
    value_part = jnp.dot(rounded, grads, preferred_element_type=F32)
    query_t = jnp.dot(keys_t, score_grad, preferred_element_type=F32)
    return query_t, key_part, value_part


def grads_kernel(info, *refs):
    rows_refs = refs[: 2 * BLOCKS]
    (stats_ref, kv_ref, kt_ref, rkv_ref, rkt_ref, dq0_ref, dq1_ref, dkv_ref, drkv_ref, q_s, g_s, dqt_s, acc, roll_acc) = refs[
        2 * BLOCKS :
    ]
    step = pl.program_id(0)

    @pl.when(step == 0)
    def _():
        acc[...] = jnp.zeros_like(acc)
        roll_acc[...] = jnp.zeros_like(roll_acc)

    load_rows(step, rows_refs, q_s, g_s)
    queries, grads = q_s[...], g_s[...]
    logs, deltas = stats_ref[:, 0, 0, :], stats_ref[:, 0, 1, :]
    top = jnp.max(logs, axis=0, keepdims=True)
    shares = jnp.exp2(logs - top)
    total = jnp.sum(shares, axis=0, keepdims=True)
    log_total = top + jnp.log2(total)
    delta = jnp.sum(shares * deltas, axis=0, keepdims=True) / total
    scores = prompt_scores(step, info, kv_ref[:, :HD], queries)
    weight_grad = lax.dot_general(kv_ref[:, HD:], grads, NT, preferred_element_type=F32)
    query_t, key_part, value_part = block_grads(scores, weight_grad, log_total, delta, queries, grads, kt_ref[...])
    dqt_s[...] = query_t
    acc[:, :HD] += key_part
    acc[:, HD:] += value_part

    @pl.when(sees_roll(step, info))
    def _():
        roll = roll_scores(step, info, rkv_ref[:, :HD], queries)
        roll_grad = lax.dot_general(rkv_ref[:, HD:], grads, NT, preferred_element_type=F32)
        query_r, key_r, value_r = block_grads(roll, roll_grad, log_total, delta, queries, grads, rkt_ref[...])
        dqt_s[...] += query_r
        roll_acc[:, :HD] += key_r
        roll_acc[:, HD:] += value_r

    out = (dqt_s[...] * SCALING).T.astype(BF16)

    @pl.when(step < BLOCKS)
    def _():
        dq0_ref[0] = out

    @pl.when(step >= BLOCKS)
    def _():
        dq1_ref[0] = out

    @pl.when(step == 2 * BLOCKS - 1)
    def _():
        dkv_ref[...] = acc[...].astype(BF16)
        drkv_ref[...] = roll_acc[...].astype(BF16)


def row_specs():
    def spec(block, part):
        return pl.BlockSpec((1, ROWS, HD), lambda i, info: (part + jnp.clip(i - 2 * block, 0, 1), 0, 0))

    return [spec(block, part) for block in range(BLOCKS) for part in (0, 2)]


def whole(*shape):
    return pl.BlockSpec(shape, lambda i, info: (0,) * len(shape))


COST = 2 * 8192 * 576 * HD


def call_stats(info, rows, kv, rkv):
    return pl.pallas_call(
        stats_kernel,
        out_shape=jax.ShapeDtypeStruct((2 * BLOCKS, 2, ROWS), F32),
        grid_spec=pltpu.PrefetchScalarGridSpec(
            num_scalar_prefetch=1,
            grid=(2 * BLOCKS,),
            in_specs=row_specs() + [whole(KEYS, 2 * HD), whole(TOKENS, 2 * HD)],
            out_specs=pl.BlockSpec((1, 2, ROWS), lambda i, info: (stats_index(i, info), 0, 0)),
            scratch_shapes=[pltpu.VMEM((ROWS, HD), BF16), pltpu.VMEM((ROWS, HD), BF16)],
        ),
        compiler_params=pltpu.CompilerParams(vmem_limit_bytes=40 * 2**20),
        cost_estimate=pl.CostEstimate(flops=2 * COST, bytes_accessed=5 * 2**20, transcendentals=8192 * 576),
        name="row_stats",
    )(info, *[r for r in rows for _ in (0, 1)], kv, rkv)


def call_grads(info, rows, stats, kv, kt, rkv, rkt):
    half = (BLOCKS, ROWS, HD)
    return pl.pallas_call(
        grads_kernel,
        out_shape=(
            jax.ShapeDtypeStruct(half, BF16),
            jax.ShapeDtypeStruct(half, BF16),
            jax.ShapeDtypeStruct((KEYS, 2 * HD), BF16),
            jax.ShapeDtypeStruct((TOKENS, 2 * HD), BF16),
        ),
        grid_spec=pltpu.PrefetchScalarGridSpec(
            num_scalar_prefetch=1,
            grid=(2 * BLOCKS,),
            in_specs=row_specs()
            + [
                pl.BlockSpec((BLOCKS, 1, 2, ROWS), lambda i, info: (0, stats_index(i, info), 0, 0)),
                whole(KEYS, 2 * HD),
                whole(HD, KEYS),
                whole(TOKENS, 2 * HD),
                whole(HD, TOKENS),
            ],
            out_specs=(
                pl.BlockSpec((1, ROWS, HD), lambda i, info: (jnp.minimum(i, BLOCKS - 1), 0, 0)),
                pl.BlockSpec((1, ROWS, HD), lambda i, info: (jnp.maximum(i - BLOCKS, 0), 0, 0)),
                whole(KEYS, 2 * HD),
                whole(TOKENS, 2 * HD),
            ),
            scratch_shapes=[
                pltpu.VMEM((ROWS, HD), BF16),
                pltpu.VMEM((ROWS, HD), BF16),
                pltpu.VMEM((HD, ROWS), F32),
                pltpu.VMEM((KEYS, 2 * HD), F32),
                pltpu.VMEM((TOKENS, 2 * HD), F32),
            ],
        ),
        compiler_params=pltpu.CompilerParams(vmem_limit_bytes=40 * 2**20),
        cost_estimate=pl.CostEstimate(flops=5 * COST, bytes_accessed=8 * 2**20, transcendentals=8192 * 576),
        name="row_grads",
    )(info, *[r for r in rows for _ in (0, 1)], stats, kv, kt, rkv, rkt)


def per_device(q_prompt, k_prompt, v_prompt, grad_prompt, q_roll, k_roll, v_roll, grad_roll, prompt_len, roll_len):
    zl, x, core = (lax.axis_index(name) for name in CTX)
    ctx = (zl * X + x) * CORES + core
    pair = jnp.transpose(jnp.concatenate([k_prompt, v_prompt], axis=-1), (1, 0, 2))
    sent = jnp.broadcast_to(pair[None], (ZL,) + pair.shape).reshape(ZL * pair.shape[0], *pair.shape[1:])
    kv = lax.all_to_all(sent, FAR, split_axis=0, concat_axis=0, tiled=True).reshape(KEYS, 2 * HD)
    token = jnp.arange(TOKENS, dtype=jnp.int32)
    roll_limit = lax.dynamic_index_in_dim(roll_len, ctx // 4, 0, keepdims=False)
    prompt_keep = (ctx * TOKENS + token < prompt_len[0]).astype(BF16)[:, None, None]
    roll_keep = ((ctx % 4) * TOKENS + token < roll_limit).astype(BF16)[:, None, None]
    own = jnp.stack([q_prompt, q_roll, grad_prompt * prompt_keep, grad_roll * roll_keep]).reshape(4, ROWS, HD)
    rows = [own] + [shifted(own, "x", steps) for steps in range(1, X)]
    rows = rows + [shifted(r, "core", 1) for r in rows]
    rkv = jnp.concatenate([k_roll, v_roll], axis=-1).reshape(TOKENS, 2 * HD)
    info = jnp.stack([x, core, zl, prompt_len[0]]).astype(jnp.int32)
    stats = call_stats(info, rows, kv, rkv)
    stats = lax.all_to_all(
        jnp.broadcast_to(stats[None], (BLOCKS,) + stats.shape), NEAR, split_axis=0, concat_axis=0, tiled=True
    )
    dq_same, dq_other, dkv, drkv = call_grads(info, rows, stats, kv, kv[:, :HD].T, rkv, rkv[:, :HD].T)
    groups = k_prompt.shape[1]
    back = lax.all_to_all(
        dkv.reshape(ZL * groups, TOKENS // groups, 2 * HD), FAR, split_axis=0, concat_axis=0, tiled=True
    )
    summed = jnp.sum(back.reshape(ZL, groups, TOKENS // groups, 2 * HD).astype(F32), axis=0)
    returned = jnp.transpose(summed.astype(BF16), (1, 0, 2))
    arrived = shifted(dq_other, "core", 1)
    halves = (dq_same.astype(F32) + arrived.astype(F32)).astype(BF16).reshape(X, 2 * ROWS, HD)
    total = halves[0].astype(F32)
    for steps in range(1, X):
        total = total + shifted(halves[steps], "x", -steps).astype(F32)
    dq = total.astype(BF16).reshape(2, TOKENS, ROWS // TOKENS, HD)
    drkv = drkv.reshape(TOKENS, 1, 2 * HD)
    return (dq[0], returned[..., :HD], returned[..., HD:], dq[1], drkv[..., :HD], drkv[..., HD:])


def solution(mesh):
    names = tuple(name for name, _ in AXES)
    fine = Mesh(mesh.devices.reshape([size for _, size in AXES]), names)
    by_head, by_token = P(CTX, GRP, None), P(CTX + GRP, None, None)
    return jax.shard_map(
        per_device,
        mesh=fine,
        in_specs=(by_head, by_token, by_token, by_head, by_head, by_head, by_head, by_head, P(), P()),
        out_specs=(by_head, by_token, by_token, by_head, by_head, by_head),
        check_vma=False,
    )
```

time: 959 us -> 147 us (0.15)
  the two profiles are of different devices: /device:TPU:8 before, /device:TPU:32 now
where the time goes in v1:
time: 147 us; the launch traced here: 146 us
  starting transfers between devices  56.7 us (39%)
  Pallas kernels  39.1 us (27%)
  waiting for transfers between devices  35.9 us (24%)
  local copies, waits for them, and re-layouts  9.15 us (6%)
  other arithmetic  3.45 us (2%)
  between operations  1.69 us (1%)
    ppermute x11, starting transfers between devices, shifted(): lax.ppermute(value, axis, [(i, (i + steps) % count) for i in range(count)])  29.7 us
    pallas_call x1, Pallas kernels, call_grads(): pl.pallas_call(grads_kernel, out_shape=(jax.ShapeDtypeStruct(half, BF16),...  24.6 us
    all_to_all x1, starting transfers between devices, per_device(): lax.all_to_all(sent, FAR, split_axis=0, concat_axis=0, tiled=True)  18.4 us
    pallas_call x1, Pallas kernels, call_stats(): pl.pallas_call(stats_kernel, out_shape=jax.ShapeDtypeStruct((2 * BLOCKS,...  14.5 us
    all_to_all x1, waiting for transfers between devices, per_device(): lax.all_to_all(dkv.reshape(ZL * groups, TOKENS // groups, 2 * HD), FAR, s...  13.2 us
    all_to_all x1, waiting for transfers between devices, per_device(): lax.all_to_all(sent, FAR, split_axis=0, concat_axis=0, tiled=True)  12.4 us
    all_to_all x1, waiting for transfers between devices, per_device(): lax.all_to_all(jnp.broadcast_to(stats[None], (BLOCKS,) + stats.shape), NE...  10.2 us
    all_to_all x1, starting transfers between devices, per_device(): lax.all_to_all(dkv.reshape(ZL * groups, TOKENS // groups, 2 * HD), FAR, s...  5.01 us
  transfers between devices with their start and end apart: 14, of which 3 were waited for; matrix products, arithmetic and copies ran while one was open for 2% of the time, Pallas kernels for 0%

profile of v1, /device:TPU:32, one launch (start us, length us, event | category | flops | bytes accessed | tf_op | source)
XLA Modules:
  0.0 146.0 jit_solution(9732969740826304079)
XLA Ops:
  1.3 1.2 dynamic_slice.4
  2.6 0.6 compare_convert_fusion
  3.2 1.2 multiply_bitcast_fusion
  4.4 1.0 pad_maximum_fusion.refs_0_.refs_1_
  5.5 4.7 %collective-permute-start.2 = (bf16[4,512,128]{2,1,0:T(8,128)(2,1)S(1)}, bf16[4,512,128]{2,1,0:T(8,128)(2,1)S(1)}, u32[]{:S(2)}, u32[]{:S(2)}) collective-permute-start(bf16[4,512,128]{2,1,0:T(8,128)(2,1)S(1)} %pad_maximum_fusion.refs_0_.refs_1_), channel_id=1, source_target_pairs={{0,48},{16,0},{32,16},{48,32},{1,49},{17,1},{33,17},{49,33},{2,50}... | collective-permute-start | bytes 1572872 | tf_op jit(solution)/shard_map/ppermute | solution.py:34
  10.2 2.7 %collective-permute-start.1 = (bf16[4,512,128]{2,1,0:T(8,128)(2,1)S(1)}, bf16[4,512,128]{2,1,0:T(8,128)(2,1)S(1)}, u32[]{:S(2)}, u32[]{:S(2)}) collective-permute-start(bf16[4,512,128]{2,1,0:T(8,128)(2,1)S(1)} %pad_maximum_fusion.refs_0_.refs_1_), channel_id=1, source_target_pairs={{0,32},{16,48},{32,0},{48,16},{1,33},{17,49},{33,1},{49,17},{2,34}... | collective-permute-start | bytes 1572872 | tf_op jit(solution)/shard_map/ppermute | solution.py:34
  12.9 2.8 %collective-permute-start = (bf16[4,512,128]{2,1,0:T(8,128)(2,1)S(1)}, bf16[4,512,128]{2,1,0:T(8,128)(2,1)S(1)}, u32[]{:S(2)}, u32[]{:S(2)}) collective-permute-start(bf16[4,512,128]{2,1,0:T(8,128)(2,1)S(1)} %pad_maximum_fusion.refs_0_.refs_1_), channel_id=1, source_target_pairs={{0,16},{16,32},{32,48},{48,0},{1,17},{17,33},{33,49},{49,1},{2,18}... | collective-permute-start | bytes 1572872 | tf_op jit(solution)/shard_map/ppermute | solution.py:34
  15.7 0.7 broadcast_in_dim.4
  16.5 18.4 %all-to-all-start = ((bf16[64,8,256]{2,1,0:T(8,128)(2,1)}), bf16[64,8,256]{2,1,0:T(8,128)(2,1)S(1)}, u32[]{:S(2)}, u32[]{:S(2)}) async-start(bf16[64,8,256]{2,1,0:T(8,128)(2,1)} %bitcast.10), calls=%async_computation | async-start | bytes 524288 | tf_op jit(solution)/shard_map/all_to_all | solution.py:259
  34.9 1.9 %collective-permute-start.3 = (bf16[4,512,128]{2,1,0:T(8,128)(2,1)S(1)}, bf16[4,512,128]{2,1,0:T(8,128)(2,1)S(1)}, u32[]{:S(2)}, u32[]{:S(2)}) collective-permute-start(bf16[4,512,128]{2,1,0:T(8,128)(2,1)S(1)} %pad_maximum_fusion.refs_0_.refs_1_), channel_id=1, source_target_pairs={{0,8},{8,0},{1,9},{9,1},{2,10},{10,2},{3,11},{11,3},{4,12},{12,4},... | collective-permute-start | bytes 1572872 | tf_op jit(solution)/shard_map/ppermute | solution.py:34
  36.8 2.4 %collective-permute-start.6 = (bf16[4,512,128]{2,1,0:T(8,128)(2,1)S(1)}, bf16[4,512,128]{2,1,0:T(8,128)(2,1)}, u32[]{:S(2)}, u32[]{:S(2)}) collective-permute-start(bf16[4,512,128]{2,1,0:T(8,128)(2,1)S(1)} %collective-permute-done.2.refs_6_.refs_7_), channel_id=1, source_target_pairs={{0,8},{8,0},{1,9},{9,1},{2,10},{10,2},{3,11},{11,3},{4,12},{12,4},... | collective-permute-start | bytes 1572872 | tf_op jit(solution)/shard_map/ppermute | solution.py:34
  39.2 1.9 %collective-permute-start.5 = (bf16[4,512,128]{2,1,0:T(8,128)(2,1)S(1)}, bf16[4,512,128]{2,1,0:T(8,128)(2,1)}, u32[]{:S(2)}, u32[]{:S(2)}) collective-permute-start(bf16[4,512,128]{2,1,0:T(8,128)(2,1)S(1)} %collective-permute-done.1.refs_4_.refs_5_), channel_id=1, source_target_pairs={{0,8},{8,0},{1,9},{9,1},{2,10},{10,2},{3,11},{11,3},{4,12},{12,4},... | collective-permute-start | bytes 1572872 | tf_op jit(solution)/shard_map/ppermute | solution.py:34
  41.2 2.4 %collective-permute-start.4 = (bf16[4,512,128]{2,1,0:T(8,128)(2,1)S(1)}, bf16[4,512,128]{2,1,0:T(8,128)(2,1)}, u32[]{:S(2)}, u32[]{:S(2)}) collective-permute-start(bf16[4,512,128]{2,1,0:T(8,128)(2,1)S(1)} %collective-permute-done.refs_2_.refs_3_), channel_id=1, source_target_pairs={{0,8},{8,0},{1,9},{9,1},{2,10},{10,2},{3,11},{11,3},{4,12},{12,4},... | collective-permute-start | bytes 1572872 | tf_op jit(solution)/shard_map/ppermute | solution.py:34
  44.1 12.4 %all-to-all-done = bf16[64,8,256]{2,1,0:T(8,128)(2,1)S(1)} async-done(((bf16[64,8,256]{2,1,0:T(8,128)(2,1)}), bf16[64,8,256]{2,1,0:T(8,128)(2,1)S(1)}, u32[]{:S(2)}, u32[]{:S(2)}) %all-to-all-start) | async-done | bytes 262176 | tf_op jit(solution)/shard_map/all_to_all | solution.py:259
  56.5 14.5 %row_stats.1 = f32[16,2,512]{2,1,0:T(2,128)S(1)} custom-call(s32[4]{0:T(128)S(1)} %pad_add_fusion.info, bf16[4,512,128]{2,1,0:T(8,128)(2,1)S(1)} %pad_maximum_fusion.refs_0_.refs_1_, bf16[4,512,128]{2,1,0:T(8,128)(2,1)S(1)} %pad_maximum_fusion.refs_0_.refs_1_, bf16[4,512,128]{2,1,0:T(8,128)(2,1)S(1)} %collective-permute-done.refs_2_.refs_3_, ...), custom_call_target="tpu_custom_call" | custom-call | flops 2415919104 | bytes 5242880 | tf_op jit(solution)/shard_map/row_stats/pallas_call | solution.py:197
  71.1 1.0 broadcast_in_dim.5
  72.0 3.6 %all-to-all-start.1 = ((f32[8,16,2,512]{3,2,1,0:T(2,128)}), f32[8,16,2,512]{3,2,1,0:T(2,128)S(1)}, u32[]{:S(2)}, u32[]{:S(2)}) async-start(f32[8,16,2,512]{3,2,1,0:T(2,128)} %broadcast_in_dim.5), calls=%async_computation.1 | async-start | bytes 1048576 | tf_op jit(solution)/shard_map/all_to_all | solution.py:270
  75.8 10.2 %all-to-all-done.1.refs_16_ = f32[8,16,2,512]{3,2,1,0:T(2,128)S(1)} async-done(((f32[8,16,2,512]{3,2,1,0:T(2,128)}), f32[8,16,2,512]{3,2,1,0:T(2,128)S(1)}, u32[]{:S(2)}, u32[]{:S(2)}) %all-to-all-start.1) | async-done | bytes 524320 | tf_op jit(solution)/shard_map/all_to_all | solution.py:270
  86.0 1.0 copy-done.1
  87.0 1.0 copy-done.3
  88.1 1.0 copy-done.5
  89.1 24.6 %row_grads.1 = (bf16[8,512,128]{2,1,0:T(8,128)(2,1)S(1)}, bf16[8,512,128]{2,1,0:T(8,128)(2,1)}, bf16[512,256]{1,0:T(8,128)(2,1)}, bf16[64,256]{1,0:T(8,128)(2,1)S(1)}) custom-call(s32[4]{0:T(128)S(1)} %pad_add_fusion.info, bf16[4,512,128]{2,1,0:T(8,128)(2,1)S(1)} %pad_maximum_fusion.refs_0_.refs_1_, ...), custom_call_target="tpu_custom_call" | custom-call | flops 6039797760 | bytes 8388608 | tf_op jit(solution)/shard_map/row_grads/pallas_call | solution.py:215
  113.7 1.9 %collective-permute-start.7 = (bf16[8,512,128]{2,1,0:T(8,128)(2,1)}, bf16[8,512,128]{2,1,0:T(8,128)(2,1)S(1)}, u32[]{:S(2)}, u32[]{:S(2)}) collective-permute-start(bf16[8,512,128]{2,1,0:T(8,128)(2,1)} %get-tuple-element.11), channel_id=1, source_target_pairs={{0,8},{8,0},{1,9},{9,1},{2,10},{10,2},{3,11},{11,3},{4,12},{12,4},... | collective-permute-start | bytes 3145736 | tf_op jit(solution)/shard_map/ppermute | solution.py:34
  115.6 5.0 %all-to-all-start.2 = ((bf16[64,8,256]{2,1,0:T(8,128)(2,1)}), bf16[64,8,256]{2,1,0:T(8,128)(2,1)S(1)}, u32[]{:S(2)}, u32[]{:S(2)}) async-start(bf16[64,8,256]{2,1,0:T(8,128)(2,1)} %bitcast.20), calls=%async_computation.2 | async-start | bytes 524288 | tf_op jit(solution)/shard_map/all_to_all | solution.py:275
  121.0 2.5 %collective-permute-start.10 = (bf16[1024,128]{1,0:T(8,128)(2,1)S(1)}, bf16[1024,128]{1,0:T(8,128)(2,1)S(1)}, u32[]{:S(2)}, u32[]{:S(2)}) collective-permute-start(bf16[1024,128]{1,0:T(8,128)(2,1)S(1)} %bitcast.43), channel_id=1, source_target_pairs={{0,16},{16,32},{32,48},{48,0},{1,17},{17,33},{33,49},{49,1},{2,18}... | collective-permute-start | bytes 786440 | tf_op jit(solution)/shard_map/ppermute | solution.py:34
  123.5 4.0 %collective-permute-start.9 = (bf16[1024,128]{1,0:T(8,128)(2,1)S(1)}, bf16[1024,128]{1,0:T(8,128)(2,1)S(1)}, u32[]{:S(2)}, u32[]{:S(2)}) collective-permute-start(bf16[1024,128]{1,0:T(8,128)(2,1)S(1)} %bitcast.42), channel_id=1, source_target_pairs={{0,32},{16,48},{32,0},{48,16},{1,33},{17,49},{33,1},{49,17},{2,34}... | collective-permute-start | bytes 786440 | tf_op jit(solution)/shard_map/ppermute | solution.py:34
  127.5 2.5 %collective-permute-start.8 = (bf16[1024,128]{1,0:T(8,128)(2,1)S(1)}, bf16[1024,128]{1,0:T(8,128)(2,1)S(1)}, u32[]{:S(2)}, u32[]{:S(2)}) collective-permute-start(bf16[1024,128]{1,0:T(8,128)(2,1)S(1)} %bitcast.41), channel_id=1, source_target_pairs={{0,48},{16,0},{32,16},{48,32},{1,49},{17,1},{33,17},{49,33},{2,50}... | collective-permute-start | bytes 786440 | tf_op jit(solution)/shard_map/ppermute | solution.py:34
  130.0 0.6 fusion.4
  130.6 13.2 %all-to-all-done.2 = bf16[64,8,256]{2,1,0:T(8,128)(2,1)S(1)} async-done(((bf16[64,8,256]{2,1,0:T(8,128)(2,1)}), bf16[64,8,256]{2,1,0:T(8,128)(2,1)S(1)}, u32[]{:S(2)}, u32[]{:S(2)}) %all-to-all-start.2) | async-done | bytes 262176 | tf_op jit(solution)/shard_map/all_to_all | solution.py:275
  143.9 0.6 copy.36
  144.5 0.6 copy.35
  145.3 0.7 slice_bitcast_fusion
  (44 shorter events, 1.2 us)
Async XLA Ops:
  0.6 15.1 %copy-start.8 = (bf16[8,8,128]{2,1,0:T(8,128)(2,1)S(1)}, bf16[8,8,128]{2,1,0:T(8,128)(2,1)}, u32[]{:S(2)}) copy-start(bf16[8,8,128]{2,1,0:T(8,128)(2,1)} %param.12) | copy-start | bytes 49156
  0.6 15.1 %copy-start.9 = (bf16[8,8,128]{2,1,0:T(8,128)(2,1)S(1)}, bf16[8,8,128]{2,1,0:T(8,128)(2,1)}, u32[]{:S(2)}) copy-start(bf16[8,8,128]{2,1,0:T(8,128)(2,1)} %param.11) | copy-start | bytes 49156
  4.4 39.2 %copy-start.6 = (bf16[64,1,128]{2,0,1:T(8,128)(2,1)S(1)}, bf16[64,1,128]{2,0,1:T(8,128)(2,1)}, u32[]{:S(2)}) copy-start(bf16[64,1,128]{2,0,1:T(8,128)(2,1)} %param.15) | copy-start | bytes 49156
  4.4 39.3 %copy-start.7 = (bf16[64,1,128]{2,0,1:T(8,128)(2,1)S(1)}, bf16[64,1,128]{2,0,1:T(8,128)(2,1)}, u32[]{:S(2)}) copy-start(bf16[64,1,128]{2,0,1:T(8,128)(2,1)} %param.16) | copy-start | bytes 49156
  5.5 31.3 %collective-permute-start.2 = (bf16[4,512,128]{2,1,0:T(8,128)(2,1)S(1)}, bf16[4,512,128]{2,1,0:T(8,128)(2,1)S(1)}, u32[]{:S(2)}, u32[]{:S(2)}) collective-permute-start(bf16[4,512,128]{2,1,0:T(8,128)(2,1)S(1)} %pad_maximum_fusion.refs_0_.refs_1_), channel_id=1, source_target_pairs={{0,48},{16,0},{32,16},{48,32},{1,49},{17,1},{33,17},{49,33},{2,50}... | collective-permute-start | bytes 1572872 | tf_op jit(solution)/shard_map/ppermute | solution.py:34
  10.2 29.0 %collective-permute-start.1 = (bf16[4,512,128]{2,1,0:T(8,128)(2,1)S(1)}, bf16[4,512,128]{2,1,0:T(8,128)(2,1)S(1)}, u32[]{:S(2)}, u32[]{:S(2)}) collective-permute-start(bf16[4,512,128]{2,1,0:T(8,128)(2,1)S(1)} %pad_maximum_fusion.refs_0_.refs_1_), channel_id=1, source_target_pairs={{0,32},{16,48},{32,0},{48,16},{1,33},{17,49},{33,1},{49,17},{2,34}... | collective-permute-start | bytes 1572872 | tf_op jit(solution)/shard_map/ppermute | solution.py:34
  12.9 28.3 %collective-permute-start = (bf16[4,512,128]{2,1,0:T(8,128)(2,1)S(1)}, bf16[4,512,128]{2,1,0:T(8,128)(2,1)S(1)}, u32[]{:S(2)}, u32[]{:S(2)}) collective-permute-start(bf16[4,512,128]{2,1,0:T(8,128)(2,1)S(1)} %pad_maximum_fusion.refs_0_.refs_1_), channel_id=1, source_target_pairs={{0,16},{16,32},{32,48},{48,0},{1,17},{17,33},{33,49},{49,1},{2,18}... | collective-permute-start | bytes 1572872 | tf_op jit(solution)/shard_map/ppermute | solution.py:34
  16.5 40.0 %all-to-all-start = ((bf16[64,8,256]{2,1,0:T(8,128)(2,1)}), bf16[64,8,256]{2,1,0:T(8,128)(2,1)S(1)}, u32[]{:S(2)}, u32[]{:S(2)}) async-start(bf16[64,8,256]{2,1,0:T(8,128)(2,1)} %bitcast.10), calls=%async_computation | async-start | bytes 524288 | tf_op jit(solution)/shard_map/all_to_all | solution.py:259
  34.9 9.2 %collective-permute-start.3 = (bf16[4,512,128]{2,1,0:T(8,128)(2,1)S(1)}, bf16[4,512,128]{2,1,0:T(8,128)(2,1)S(1)}, u32[]{:S(2)}, u32[]{:S(2)}) collective-permute-start(bf16[4,512,128]{2,1,0:T(8,128)(2,1)S(1)} %pad_maximum_fusion.refs_0_.refs_1_), channel_id=1, source_target_pairs={{0,8},{8,0},{1,9},{9,1},{2,10},{10,2},{3,11},{11,3},{4,12},{12,4},... | collective-permute-start | bytes 1572872 | tf_op jit(solution)/shard_map/ppermute | solution.py:34
  36.8 19.7 %collective-permute-start.6 = (bf16[4,512,128]{2,1,0:T(8,128)(2,1)S(1)}, bf16[4,512,128]{2,1,0:T(8,128)(2,1)}, u32[]{:S(2)}, u32[]{:S(2)}) collective-permute-start(bf16[4,512,128]{2,1,0:T(8,128)(2,1)S(1)} %collective-permute-done.2.refs_6_.refs_7_), channel_id=1, source_target_pairs={{0,8},{8,0},{1,9},{9,1},{2,10},{10,2},{3,11},{11,3},{4,12},{12,4},... | collective-permute-start | bytes 1572872 | tf_op jit(solution)/shard_map/ppermute | solution.py:34
  39.2 31.8 %copy-start = (bf16[4,512,128]{2,1,0:T(8,128)(2,1)}, bf16[4,512,128]{2,1,0:T(8,128)(2,1)S(1)}, u32[]{:S(2)}) copy-start(bf16[4,512,128]{2,1,0:T(8,128)(2,1)S(1)} %collective-permute-done.1.refs_4_.refs_5_) | copy-start | bytes 1572868
  39.2 17.3 %collective-permute-start.5 = (bf16[4,512,128]{2,1,0:T(8,128)(2,1)S(1)}, bf16[4,512,128]{2,1,0:T(8,128)(2,1)}, u32[]{:S(2)}, u32[]{:S(2)}) collective-permute-start(bf16[4,512,128]{2,1,0:T(8,128)(2,1)S(1)} %collective-permute-done.1.refs_4_.refs_5_), channel_id=1, source_target_pairs={{0,8},{8,0},{1,9},{9,1},{2,10},{10,2},{3,11},{11,3},{4,12},{12,4},... | collective-permute-start | bytes 1572872 | tf_op jit(solution)/shard_map/ppermute | solution.py:34
  41.2 29.9 %copy-start.2 = (bf16[4,512,128]{2,1,0:T(8,128)(2,1)}, bf16[4,512,128]{2,1,0:T(8,128)(2,1)S(1)}, u32[]{:S(2)}) copy-start(bf16[4,512,128]{2,1,0:T(8,128)(2,1)S(1)} %collective-permute-done.refs_2_.refs_3_) | copy-start | bytes 1572868
  41.2 15.3 %collective-permute-start.4 = (bf16[4,512,128]{2,1,0:T(8,128)(2,1)S(1)}, bf16[4,512,128]{2,1,0:T(8,128)(2,1)}, u32[]{:S(2)}, u32[]{:S(2)}) collective-permute-start(bf16[4,512,128]{2,1,0:T(8,128)(2,1)S(1)} %collective-permute-done.refs_2_.refs_3_), channel_id=1, source_target_pairs={{0,8},{8,0},{1,9},{9,1},{2,10},{10,2},{3,11},{11,3},{4,12},{12,4},... | collective-permute-start | bytes 1572872 | tf_op jit(solution)/shard_map/ppermute | solution.py:34
  44.1 27.0 %copy-start.4 = (bf16[4,512,128]{2,1,0:T(8,128)(2,1)}, bf16[4,512,128]{2,1,0:T(8,128)(2,1)S(1)}, u32[]{:S(2)}) copy-start(bf16[4,512,128]{2,1,0:T(8,128)(2,1)S(1)} %collective-permute-done.3.refs_8_.refs_9_) | copy-start | bytes 1572868
  72.0 14.0 %all-to-all-start.1 = ((f32[8,16,2,512]{3,2,1,0:T(2,128)}), f32[8,16,2,512]{3,2,1,0:T(2,128)S(1)}, u32[]{:S(2)}, u32[]{:S(2)}) async-start(f32[8,16,2,512]{3,2,1,0:T(2,128)} %broadcast_in_dim.5), calls=%async_computation.1 | async-start | bytes 1048576 | tf_op jit(solution)/shard_map/all_to_all | solution.py:270
  86.0 1.0 copy-start.1
  87.0 1.0 copy-start.3
  88.1 1.0 copy-start.5
  113.7 6.9 %collective-permute-start.7 = (bf16[8,512,128]{2,1,0:T(8,128)(2,1)}, bf16[8,512,128]{2,1,0:T(8,128)(2,1)S(1)}, u32[]{:S(2)}, u32[]{:S(2)}) collective-permute-start(bf16[8,512,128]{2,1,0:T(8,128)(2,1)} %get-tuple-element.11), channel_id=1, source_target_pairs={{0,8},{8,0},{1,9},{9,1},{2,10},{10,2},{3,11},{11,3},{4,12},{12,4},... | collective-permute-start | bytes 3145736 | tf_op jit(solution)/shard_map/ppermute | solution.py:34
  115.6 28.2 %all-to-all-start.2 = ((bf16[64,8,256]{2,1,0:T(8,128)(2,1)}), bf16[64,8,256]{2,1,0:T(8,128)(2,1)S(1)}, u32[]{:S(2)}, u32[]{:S(2)}) async-start(bf16[64,8,256]{2,1,0:T(8,128)(2,1)} %bitcast.20), calls=%async_computation.2 | async-start | bytes 524288 | tf_op jit(solution)/shard_map/all_to_all | solution.py:275
  121.0 24.1 %collective-permute-start.10 = (bf16[1024,128]{1,0:T(8,128)(2,1)S(1)}, bf16[1024,128]{1,0:T(8,128)(2,1)S(1)}, u32[]{:S(2)}, u32[]{:S(2)}) collective-permute-start(bf16[1024,128]{1,0:T(8,128)(2,1)S(1)} %bitcast.43), channel_id=1, source_target_pairs={{0,16},{16,32},{32,48},{48,0},{1,17},{17,33},{33,49},{49,1},{2,18}... | collective-permute-start | bytes 786440 | tf_op jit(solution)/shard_map/ppermute | solution.py:34
  123.5 21.6 %collective-permute-start.9 = (bf16[1024,128]{1,0:T(8,128)(2,1)S(1)}, bf16[1024,128]{1,0:T(8,128)(2,1)S(1)}, u32[]{:S(2)}, u32[]{:S(2)}) collective-permute-start(bf16[1024,128]{1,0:T(8,128)(2,1)S(1)} %bitcast.42), channel_id=1, source_target_pairs={{0,32},{16,48},{32,0},{48,16},{1,33},{17,49},{33,1},{49,17},{2,34}... | collective-permute-start | bytes 786440 | tf_op jit(solution)/shard_map/ppermute | solution.py:34
  127.5 17.6 %collective-permute-start.8 = (bf16[1024,128]{1,0:T(8,128)(2,1)S(1)}, bf16[1024,128]{1,0:T(8,128)(2,1)S(1)}, u32[]{:S(2)}, u32[]{:S(2)}) collective-permute-start(bf16[1024,128]{1,0:T(8,128)(2,1)S(1)} %bitcast.41), channel_id=1, source_target_pairs={{0,48},{16,0},{32,16},{48,32},{1,49},{17,1},{33,17},{49,33},{2,50}... | collective-permute-start | bytes 786440 | tf_op jit(solution)/shard_map/ppermute | solution.py:34

commit v2 on v1

v2 whole, which is shorter than its diff:
```python
import math

import jax
import jax.numpy as jnp
from jax import lax
from jax.experimental import pallas as pl
from jax.experimental.pallas import tpu as pltpu
from jax.sharding import Mesh, PartitionSpec as P

AXES = (("zl", 8), ("x", 4), ("core", 2), ("zh", 2), ("y", 4))
CTX = ("zl", "x", "core")
GRP = ("zh", "y")
FAR = ("zl", "zh", "y")
NEAR = ("x", "core")
X, CORES, ZL = 4, 2, 8
BLOCKS = X * CORES

HD = 128
TOKENS = 64
ROWS = 512
KEYS = ZL * TOKENS
MASKED = -1e30
SCALING = 1.0 / math.sqrt(HD)
LOG2E = math.log2(math.e)
SCALE2 = SCALING * LOG2E
F32 = jnp.float32
BF16 = jnp.bfloat16
NT = (((1,), (1,)), ((), ()))


def shifted(value, axis, steps):
    count = lax.axis_size(axis)
    return lax.ppermute(value, axis, [(i, (i + steps) % count) for i in range(count)])


def owner(block, info):
    return (info[0] + X - block % X) % X, (info[1] + block // X) % CORES


def first_tokens(block, kind, info):
    owner_x, owner_core = owner(block, info)
    in_prompt = ((info[2] * X + owner_x) * CORES + owner_core) * TOKENS
    in_roll = ((owner_x % 2) * CORES + owner_core) * TOKENS
    roll = kind == 1
    return jnp.where(roll, in_roll, in_prompt), jnp.where(roll, info[4 + info[2] * 2 + owner_x // 2], info[3])


def row_tokens():
    return lax.broadcasted_iota(jnp.int32, (1, ROWS), 1) // 8


def prompt_scores(block, kind, info, keys, queries):
    scores = lax.dot_general(keys, queries, NT, preferred_element_type=F32) * SCALE2
    key = lax.broadcasted_iota(jnp.int32, (KEYS, 1), 0)
    key_pos = (key // TOKENS) * (BLOCKS * TOKENS) + key % TOKENS + (info[0] * CORES + info[1]) * TOKENS
    limit = jnp.where(kind == 1, info[3] - 1, first_tokens(block, 0, info)[0] + row_tokens())
    return jnp.where(key_pos <= limit, scores, MASKED)


def roll_scores(block, info, keys, queries):
    scores = lax.dot_general(keys, queries, NT, preferred_element_type=F32) * SCALE2
    key_pos = lax.broadcasted_iota(jnp.int32, (TOKENS, 1), 0) + ((info[0] % 2) * CORES + info[1]) * TOKENS
    return jnp.where(key_pos <= first_tokens(block, 1, info)[0] + row_tokens(), scores, MASKED)


def partial_stats(scores, weight_grad):
    top = jnp.max(scores, axis=0, keepdims=True)
    weights = jnp.exp2(scores - top)
    total = jnp.sum(weights, axis=0, keepdims=True)
    product = jnp.sum(weights * weight_grad, axis=0, keepdims=True)
    return top + jnp.log2(total), product / total


def merged(first, second):
    (log_a, delta_a), (log_b, delta_b) = first, second
    top = jnp.maximum(log_a, log_b)
    share_a, share_b = jnp.exp2(log_a - top), jnp.exp2(log_b - top)
    total = share_a + share_b
    return top + jnp.log2(total), (delta_a * share_a + delta_b * share_b) / total


def fetch(refs, rows_s, sems):
    for i, ref in enumerate(refs):
        pltpu.make_async_copy(ref, rows_s.at[i], sems.at[i]).start()


def arrive(i, refs, rows_s, sems):
    pltpu.make_async_copy(refs[0], rows_s.at[i], sems.at[i]).wait()


def sees_roll(block, kind, info):
    return (kind == 1) & (owner(block, info)[0] // 2 == info[0] // 2)


def block_stats(block, kind, info, queries, grads, kv_ref, rk_ref, rv_ref, out_ref):
    def put(stats):
        out_ref[pl.ds(2 * kind, 1), :] = stats[0]
        out_ref[pl.ds(2 * kind + 1, 1), :] = stats[1]

    scores = prompt_scores(block, kind, info, kv_ref[:, :HD], queries)
    weight_grad = lax.dot_general(kv_ref[:, HD:], grads, NT, preferred_element_type=F32)
    stats = partial_stats(scores, weight_grad)
    put(stats)

    @pl.when(sees_roll(block, kind, info))
    def _():
        roll = roll_scores(block, info, rk_ref[...], queries)
        roll_grad = lax.dot_general(rv_ref[...], grads, NT, preferred_element_type=F32)
        put(merged(stats, partial_stats(roll, roll_grad)))


def own_stats_kernel(info, rows_ref, kv_ref, rk_ref, rv_ref, stats_ref):
    @pl.loop(0, 2)
    def _(kind):
        block_stats(0, kind, info, rows_ref[kind], rows_ref[2 + kind], kv_ref, rk_ref, rv_ref, stats_ref)


def stats_kernel(info, *refs):
    others, (own_ref, kv_ref, rk_ref, rv_ref, out_ref, rows_s, stats_s, sems) = refs[: BLOCKS - 1], refs[BLOCKS - 1 :]
    fetch(others, rows_s, sems)
    stats_s[info[0] * CORES + info[1]] = own_ref[...]

    @pl.loop(2, 2 * BLOCKS)
    def _(step):
        block, kind = step // 2, step % 2

        @pl.when(kind == 0)
        def _():
            arrive(block - 1, others, rows_s, sems)

        owner_x, owner_core = owner(block, info)
        rows = rows_s.at[block - 1]
        out = stats_s.at[owner_x * CORES + owner_core]
        block_stats(block, kind, info, rows[kind], rows[2 + kind], kv_ref, rk_ref, rv_ref, out)

    for peer in range(BLOCKS):
        out_ref[peer] = stats_s[...]


def combined(stats_ref, block, kind, info):
    owner_x, owner_core = owner(block, info)
    at = owner_x * CORES + owner_core
    logs = jnp.concatenate([stats_ref[i, at, pl.ds(2 * kind, 1), :] for i in range(BLOCKS)], axis=0)
    deltas = jnp.concatenate([stats_ref[i, at, pl.ds(2 * kind + 1, 1), :] for i in range(BLOCKS)], axis=0)
    top = jnp.max(logs, axis=0, keepdims=True)
    shares = jnp.exp2(logs - top)
    total = jnp.sum(shares, axis=0, keepdims=True)
    start, length = first_tokens(block, kind, info)
    log_total = jnp.where(start + row_tokens() < length, top + jnp.log2(total), -MASKED)
    return log_total, jnp.sum(shares * deltas, axis=0, keepdims=True) / total


def block_grads(scores, weight_grad, log_total, delta, queries, grads, keys_t):
    weights = jnp.exp2(scores - log_total)
    score_grad = (weights * (weight_grad - delta)).astype(BF16)
    key_part = jnp.dot(score_grad, queries, preferred_element_type=F32)
    value_part = jnp.dot(weights.astype(BF16), grads, preferred_element_type=F32)
    query_t = jnp.dot(keys_t, score_grad, preferred_element_type=F32)
    return query_t, key_part, value_part


def grads_kernel(info, *refs):
    rows = refs[:BLOCKS]
    (stats_ref, kv_ref, kt_ref, rk_ref, rkt_ref, rv_ref) = refs[BLOCKS : BLOCKS + 6]
    (dq0_ref, dq1_ref, dkv_ref, drk_ref, drv_ref, rows_s, dqt_s, acc, roll_acc, sems) = refs[BLOCKS + 6 :]
    fetch(rows, rows_s, sems)
    acc[...] = jnp.zeros_like(acc)
    roll_acc[...] = jnp.zeros_like(roll_acc)

    @pl.loop(0, 2 * BLOCKS)
    def _(step):
        block, kind = step // 2, step % 2

        @pl.when(kind == 0)
        def _():
            arrive(block, rows, rows_s, sems)

        log_total, delta = combined(stats_ref, block, kind, info)
        queries, grads = rows_s[block, kind], rows_s[block, 2 + kind]
        scores = prompt_scores(block, kind, info, kv_ref[:, :HD], queries)
        weight_grad = lax.dot_general(kv_ref[:, HD:], grads, NT, preferred_element_type=F32)
        query_t, key_part, value_part = block_grads(
            scores, weight_grad, log_total, delta, queries, grads, kt_ref[...]
        )
        dqt_s[...] = query_t
        acc[:, :HD] += key_part
        acc[:, HD:] += value_part

        @pl.when(sees_roll(block, kind, info))
        def _():
            roll = roll_scores(block, info, rk_ref[...], queries)
            roll_grad = lax.dot_general(rv_ref[...], grads, NT, preferred_element_type=F32)
            query_r, key_r, value_r = block_grads(roll, roll_grad, log_total, delta, queries, grads, rkt_ref[...])
            dqt_s[...] += query_r
            roll_acc[:, :HD] += key_r
            roll_acc[:, HD:] += value_r

        out = (dqt_s[...] * SCALING).T.astype(BF16)
        at = pl.ds(pl.multiple_of(kind * ROWS, ROWS), ROWS)

        @pl.when(block < X)
        def _():
            dq0_ref[block, at, :] = out

        @pl.when(block >= X)
        def _():
            dq1_ref[block - X, at, :] = out

    dkv_ref[:, :HD] = (acc[:, :HD] * SCALING).astype(BF16)
    dkv_ref[:, HD:] = acc[:, HD:].astype(BF16)
    drk_ref[...] = (roll_acc[:, :HD] * SCALING).astype(BF16)
    drv_ref[...] = roll_acc[:, HD:].astype(BF16)


def finish_kernel(back_ref, dk_ref, dv_ref):
    total = jnp.sum(back_ref[...].astype(F32), axis=0)
    for head in range(total.shape[0]):
        dk_ref[:, head, :] = total[head, :, :HD].astype(BF16)
        dv_ref[:, head, :] = total[head, :, HD:].astype(BF16)


VMEM = pl.BlockSpec(memory_space=pltpu.VMEM)
SMEM = pl.BlockSpec(memory_space=pltpu.SMEM)
ANY = pl.BlockSpec(memory_space=pl.ANY)
PARAMS = pltpu.CompilerParams(vmem_limit_bytes=28 * 2**20)
COST = 2 * 1024 * 576 * HD


def cost(flops, byte_count):
    return pl.CostEstimate(flops=flops, bytes_accessed=byte_count, transcendentals=0)


def call_own_stats(info, own, kv, rk, rv):
    return pl.pallas_call(
        own_stats_kernel,
        out_shape=jax.ShapeDtypeStruct((4, ROWS), F32),
        in_specs=[SMEM] + [VMEM] * 4,
        out_specs=VMEM,
        compiler_params=PARAMS,
        cost_estimate=cost(OWN_FLOPS, 2**20),
        name="row_own_stats",
    )(info, own, kv, rk, rv)


OWN_FLOPS = 100 * 10**9


def call_stats(info, others, own_stats, kv, rk, rv):
    return pl.pallas_call(
        stats_kernel,
        out_shape=jax.ShapeDtypeStruct((BLOCKS, BLOCKS, 4, ROWS), F32),
        in_specs=[SMEM] + [ANY] * (BLOCKS - 1) + [VMEM] * 4,
        out_specs=VMEM,
        scratch_shapes=[
            pltpu.VMEM((BLOCKS - 1, 4, ROWS, HD), BF16),
            pltpu.VMEM((BLOCKS, 4, ROWS), F32),
            pltpu.SemaphoreType.DMA((BLOCKS - 1,)),
        ],
        compiler_params=PARAMS,
        cost_estimate=cost(2 * 7 * COST, 4 * 2**20),
        name="row_stats",
    )(info, *others, own_stats, kv, rk, rv)


def call_grads(info, rows, stats, kv, kt, rk, rkt, rv):
    half = jax.ShapeDtypeStruct((X, 2 * ROWS, HD), BF16)
    roll = jax.ShapeDtypeStruct((TOKENS, HD), BF16)
    return pl.pallas_call(
        grads_kernel,
        out_shape=(half, half, jax.ShapeDtypeStruct((KEYS, 2 * HD), BF16), roll, roll),
        in_specs=[SMEM] + [ANY] * BLOCKS + [VMEM] * 6,
        out_specs=(VMEM,) * 5,
        scratch_shapes=[
            pltpu.VMEM((BLOCKS, 4, ROWS, HD), BF16),
            pltpu.VMEM((HD, ROWS), F32),
            pltpu.VMEM((KEYS, 2 * HD), F32),
            pltpu.VMEM((TOKENS, 2 * HD), F32),
            pltpu.SemaphoreType.DMA((BLOCKS,)),
        ],
        compiler_params=PARAMS,
        cost_estimate=cost(5 * 8 * COST, 7 * 2**20),
        name="row_grads",
    )(info, *rows, stats, kv, kt, rk, rkt, rv)


def call_finish(back):
    tokens, heads = back.shape[2], back.shape[1]
    out = jax.ShapeDtypeStruct((tokens, heads, HD), BF16)
    return pl.pallas_call(
        finish_kernel, out_shape=(out, out), in_specs=[VMEM], out_specs=(VMEM, VMEM), name="sum_planes"
    )(back)


def per_device(q_prompt, k_prompt, v_prompt, grad_prompt, q_roll, k_roll, v_roll, grad_roll, prompt_len, roll_len):
    zl, x, core = (lax.axis_index(name) for name in CTX)
    pair = jnp.transpose(jnp.concatenate([k_prompt, v_prompt], axis=-1), (1, 0, 2))
    sent = jnp.broadcast_to(pair[None], (ZL,) + pair.shape).reshape(ZL * pair.shape[0], *pair.shape[1:])
    kv = lax.all_to_all(sent, FAR, split_axis=0, concat_axis=0, tiled=True).reshape(KEYS, 2 * HD)
    own = jnp.stack([q_prompt, q_roll, grad_prompt, grad_roll]).reshape(4, ROWS, HD)
    rows = [own] + [shifted(own, "x", steps) for steps in range(1, X)]
    rows = rows + [shifted(r, "core", 1) for r in rows]
    rk, rv = k_roll.reshape(TOKENS, HD), v_roll.reshape(TOKENS, HD)
    info = jnp.concatenate([jnp.stack([x, core, zl]).astype(jnp.int32), prompt_len, roll_len])
    own_stats = call_own_stats(info, own, kv, rk, rv)
    stats = call_stats(info, rows[1:], own_stats, kv, rk, rv)
    stats = lax.all_to_all(stats, NEAR, split_axis=0, concat_axis=0, tiled=True)
    dq_same, dq_other, dkv, drk, drv = call_grads(info, rows, stats, kv, kv[:, :HD].T, rk, rk.T, rv)
    groups = k_prompt.shape[1]
    back = lax.all_to_all(
        dkv.reshape(ZL * groups, TOKENS // groups, 2 * HD), FAR, split_axis=0, concat_axis=0, tiled=True
    )
    dk_prompt, dv_prompt = call_finish(back.reshape(ZL, groups, TOKENS // groups, 2 * HD))
    arrived = shifted(dq_other, "core", 1)
    halves = (dq_same.astype(F32) + arrived.astype(F32)).astype(BF16)
    parts = [halves[0]] + [shifted(halves[steps], "x", -steps) for steps in range(1, X)]
    dq = [
        sum(part[first : first + ROWS].astype(F32) for part in parts).astype(BF16).reshape(q_prompt.shape)
        for first in (0, ROWS)
    ]
    return (dq[0], dk_prompt, dv_prompt, dq[1], drk.reshape(k_roll.shape), drv.reshape(v_roll.shape))


def solution(mesh):
    names = tuple(name for name, _ in AXES)
    fine = Mesh(mesh.devices.reshape([size for _, size in AXES]), names)
    by_head, by_token = P(CTX, GRP, None), P(CTX + GRP, None, None)
    return jax.shard_map(
        per_device,
        mesh=fine,
        in_specs=(by_head, by_token, by_token, by_head, by_head, by_head, by_head, by_head, P(), P()),
        out_specs=(by_head, by_token, by_token, by_head, by_head, by_head),
        check_vma=False,
    )
```

time: 147 us -> 149 us (1.014)
  starting transfers between devices: 56.7 us -> 65.8 us
  Pallas kernels: 39.1 us -> 33.7 us
  local copies, waits for them, and re-layouts: 9.15 us -> 4.96 us
  waiting for transfers between devices: 35.9 us -> 39.5 us
    ppermute x11, waiting for transfers between devices: 0.03 us -> 15 us  [shifted(): lax.ppermute(value, axis, [(i, (i + steps) % count) for i in range(count)])]
    all_to_all x1, waiting for transfers between devices: 12.4 us -> 0.01 us  [per_device(): lax.all_to_all(sent, FAR, split_axis=0, concat_axis=0, tiled=True)]
    all_to_all x1, starting transfers between devices: 5.01 us -> 15 us  [per_device(): lax.all_to_all(dkv.reshape(ZL * groups, TOKENS // groups, 2 * HD), FAR, s...]
    pallas_call x2 -> x4, Pallas kernels: 39.1 us -> 33.7 us  [the longest x1 20.2 us: call_grads(): pl.pallas_call(grads_kernel, out_shape=(half, half, jax.ShapeDtypeStruct(...]
    another operation x3 -> x1, other arithmetic: 2.29 us -> 0.07 us  [per_device(): jnp.stack([q_prompt, q_roll, grad_prompt, grad_roll]).reshape(4, ROWS, HD)]
    unnamed x25 -> x30, local copies, waits for them, and re-layouts: 4.72 us -> 4.08 us
  transfers between devices with their start and end apart: 14 -> 14, of which waited for: 3 -> 5; matrix products, arithmetic and copies ran while one was open for 2% -> 0% of each run, Pallas kernels for 0% -> 2%
where the time goes in v2:
time: 149 us; the launch traced here: 148 us
  starting transfers between devices  65.8 us (44%)
  waiting for transfers between devices  39.5 us (27%)
  Pallas kernels  33.7 us (23%)
  local copies, waits for them, and re-layouts  4.96 us (3%)
  other arithmetic  2.02 us (1%)
  between operations  1.66 us (1%)
    ppermute x11, starting transfers between devices, shifted(): lax.ppermute(value, axis, [(i, (i + steps) % count) for i in range(count)])  28.6 us
    pallas_call x1, Pallas kernels, call_grads(): pl.pallas_call(grads_kernel, out_shape=(half, half, jax.ShapeDtypeStruct(...  20.2 us
    all_to_all x1, starting transfers between devices, per_device(): lax.all_to_all(sent, FAR, split_axis=0, concat_axis=0, tiled=True)  18.4 us
    ppermute x11, waiting for transfers between devices, shifted(): lax.ppermute(value, axis, [(i, (i + steps) % count) for i in range(count)])  15 us
    all_to_all x1, starting transfers between devices, per_device(): lax.all_to_all(dkv.reshape(ZL * groups, TOKENS // groups, 2 * HD), FAR, s...  15 us
    all_to_all x1, waiting for transfers between devices, per_device(): lax.all_to_all(dkv.reshape(ZL * groups, TOKENS // groups, 2 * HD), FAR, s...  14.4 us
    all_to_all x1, waiting for transfers between devices, per_device(): stats = lax.all_to_all(stats, NEAR, split_axis=0, concat_axis=0, tiled=True)  10.1 us
    pallas_call x1, Pallas kernels, call_stats(): pl.pallas_call(stats_kernel, out_shape=jax.ShapeDtypeStruct((BLOCKS, BLOC...  10 us
  transfers between devices with their start and end apart: 14, of which 5 were waited for; matrix products, arithmetic and copies ran while one was open for 0% of the time, Pallas kernels for 2%

profile of v2, /device:TPU:32, one launch (start us, length us, event | category | flops | bytes accessed | tf_op | source)
XLA Modules:
  0.0 147.7 jit_solution(15835051594399711959)
XLA Ops:
  0.7 0.8 maximum_bitcast_fusion
  1.6 0.7 broadcast_in_dim.2
  2.3 18.4 %all-to-all-start = ((bf16[64,8,256]{2,1,0:T(8,128)(2,1)}), bf16[64,8,256]{2,1,0:T(8,128)(2,1)S(1)}, u32[]{:S(2)}, u32[]{:S(2)}) async-start(bf16[64,8,256]{2,1,0:T(8,128)(2,1)} %bitcast.8), calls=%async_computation | async-start | bytes 524288 | tf_op jit(solution)/shard_map/all_to_all | solution.py:298
  20.8 4.7 %collective-permute-start.2 = (bf16[4,512,128]{2,1,0:T(8,128)(2,1)S(1)}, bf16[4,512,128]{2,1,0:T(8,128)(2,1)S(1)}, u32[]{:S(2)}, u32[]{:S(2)}) collective-permute-start(bf16[4,512,128]{2,1,0:T(8,128)(2,1)S(1)} %pad_maximum_fusion.rows_ref.refs_0_), channel_id=1, source_target_pairs={{0,48},{16,0},{32,16},{48,32},{1,49},{17,1},{33,17},{49,33},{2,50}... | collective-permute-start | bytes 1572872 | tf_op jit(solution)/shard_map/ppermute | solution.py:33
  25.5 2.7 %collective-permute-start.1 = (bf16[4,512,128]{2,1,0:T(8,128)(2,1)S(1)}, bf16[4,512,128]{2,1,0:T(8,128)(2,1)S(1)}, u32[]{:S(2)}, u32[]{:S(2)}) collective-permute-start(bf16[4,512,128]{2,1,0:T(8,128)(2,1)S(1)} %pad_maximum_fusion.rows_ref.refs_0_), channel_id=1, source_target_pairs={{0,32},{16,48},{32,0},{48,16},{1,33},{17,49},{33,1},{49,17},{2,34}... | collective-permute-start | bytes 1572872 | tf_op jit(solution)/shard_map/ppermute | solution.py:33
  28.2 2.8 %collective-permute-start = (bf16[4,512,128]{2,1,0:T(8,128)(2,1)S(1)}, bf16[4,512,128]{2,1,0:T(8,128)(2,1)S(1)}, u32[]{:S(2)}, u32[]{:S(2)}) collective-permute-start(bf16[4,512,128]{2,1,0:T(8,128)(2,1)S(1)} %pad_maximum_fusion.rows_ref.refs_0_), channel_id=1, source_target_pairs={{0,16},{16,32},{32,48},{48,0},{1,17},{17,33},{33,49},{49,1},{2,18}... | collective-permute-start | bytes 1572872 | tf_op jit(solution)/shard_map/ppermute | solution.py:33
  31.0 1.9 %collective-permute-start.3 = (bf16[4,512,128]{2,1,0:T(8,128)(2,1)S(1)}, bf16[4,512,128]{2,1,0:T(8,128)(2,1)S(1)}, u32[]{:S(2)}, u32[]{:S(2)}) collective-permute-start(bf16[4,512,128]{2,1,0:T(8,128)(2,1)S(1)} %pad_maximum_fusion.rows_ref.refs_0_), channel_id=1, source_target_pairs={{0,8},{8,0},{1,9},{9,1},{2,10},{10,2},{3,11},{11,3},{4,12},{12,4},... | collective-permute-start | bytes 1572872 | tf_op jit(solution)/shard_map/ppermute | solution.py:33
  33.7 13.7 %collective-permute-done.2.refs_2_.refs_3_ = bf16[4,512,128]{2,1,0:T(8,128)(2,1)S(1)} collective-permute-done((bf16[4,512,128]{2,1,0:T(8,128)(2,1)S(1)}, bf16[4,512,128]{2,1,0:T(8,128)(2,1)S(1)}, u32[]{:S(2)}, u32[]{:S(2)}) %collective-permute-start.2) | collective-permute-done | bytes 524320 | tf_op jit(solution)/shard_map/ppermute | solution.py:33
  47.3 1.9 %collective-permute-start.6 = (bf16[4,512,128]{2,1,0:T(8,128)(2,1)S(1)}, bf16[4,512,128]{2,1,0:T(8,128)(2,1)}, u32[]{:S(2)}, u32[]{:S(2)}) collective-permute-start(bf16[4,512,128]{2,1,0:T(8,128)(2,1)S(1)} %collective-permute-done.2.refs_2_.refs_3_), channel_id=1, source_target_pairs={{0,8},{8,0},{1,9},{9,1},{2,10},{10,2},{3,11},{11,3},{4,12},{12,4},... | collective-permute-start | bytes 1572872 | tf_op jit(solution)/shard_map/ppermute | solution.py:33
  49.3 2.4 %collective-permute-start.5 = (bf16[4,512,128]{2,1,0:T(8,128)(2,1)S(1)}, bf16[4,512,128]{2,1,0:T(8,128)(2,1)}, u32[]{:S(2)}, u32[]{:S(2)}) collective-permute-start(bf16[4,512,128]{2,1,0:T(8,128)(2,1)S(1)} %collective-permute-done.1.refs_1_.refs_2_), channel_id=1, source_target_pairs={{0,8},{8,0},{1,9},{9,1},{2,10},{10,2},{3,11},{11,3},{4,12},{12,4},... | collective-permute-start | bytes 1572872 | tf_op jit(solution)/shard_map/ppermute | solution.py:33
  51.7 1.2 collective-permute-done.refs_0_.refs_1_
  52.9 1.9 %collective-permute-start.4 = (bf16[4,512,128]{2,1,0:T(8,128)(2,1)S(1)}, bf16[4,512,128]{2,1,0:T(8,128)(2,1)}, u32[]{:S(2)}, u32[]{:S(2)}) collective-permute-start(bf16[4,512,128]{2,1,0:T(8,128)(2,1)S(1)} %collective-permute-done.refs_0_.refs_1_), channel_id=1, source_target_pairs={{0,8},{8,0},{1,9},{9,1},{2,10},{10,2},{3,11},{11,3},{4,12},{12,4},... | collective-permute-start | bytes 1572872 | tf_op jit(solution)/shard_map/ppermute | solution.py:33
  54.9 1.8 %row_own_stats.1.refs_7_ = f32[4,512]{1,0:T(4,128)S(1)} custom-call(s32[20]{0:T(128)S(1)} %concatenate.7.info, bf16[4,512,128]{2,1,0:T(8,128)(2,1)S(1)} %pad_maximum_fusion.rows_ref.refs_0_, bf16[512,256]{1,0:T(8,128)(2,1)S(1)} %bitcast.41, bf16[64,128]{1,0:T(8,128)(2,1)S(1)} %bitcast.47, bf16[64,128]{1,0:T(8,128)(2,1)S(1)} %bitcast.50), custom_call_target="tpu_custom_call" | custom-call | flops 99999997952 | bytes 1048576 | tf_op jit(solution)/shard_map/row_own_stats/pallas_call | solution.py:234
  56.8 10.0 %row_stats.1 = f32[8,8,4,512]{3,2,1,0:T(4,128)} custom-call(s32[20]{0:T(128)S(1)} %concatenate.7.info, bf16[4,512,128]{2,1,0:T(8,128)(2,1)S(1)} %collective-permute-done.refs_0_.refs_1_, bf16[4,512,128]{2,1,0:T(8,128)(2,1)S(1)} %collective-permute-done.1.refs_1_.refs_2_, bf16[4,512,128]{2,1,0:T(8,128)(2,1)S(1)} %collective-permute-done.2.refs_2_.refs_3_, ...), custom_call_target="tpu_custom_call" | custom-call | flops 2113929216 | bytes 4194304 | tf_op jit(solution)/shard_map/row_stats/pallas_call | solution.py:249
  66.9 3.8 %all-to-all-start.1 = ((f32[8,8,4,512]{3,2,1,0:T(4,128)}), f32[8,8,4,512]{3,2,1,0:T(4,128)S(1)}, u32[]{:S(2)}, u32[]{:S(2)}) async-start(f32[8,8,4,512]{3,2,1,0:T(4,128)} %row_stats.1), calls=%async_computation.1 | async-start | bytes 1048576 | tf_op jit(solution)/shard_map/all_to_all | solution.py:306
  70.7 0.1 copy.25
  70.8 0.1 copy.31
  70.9 10.1 %all-to-all-done.1.refs_8_ = f32[8,8,4,512]{3,2,1,0:T(4,128)S(1)} async-done(((f32[8,8,4,512]{3,2,1,0:T(4,128)}), f32[8,8,4,512]{3,2,1,0:T(4,128)S(1)}, u32[]{:S(2)}, u32[]{:S(2)}) %all-to-all-start.1) | async-done | bytes 524320 | tf_op jit(solution)/shard_map/all_to_all | solution.py:306
  81.0 1.0 copy-done.2
  82.1 1.0 copy-done.4
  83.1 1.0 copy-done.6
  84.2 20.2 %row_grads.1 = (bf16[4,1024,128]{2,1,0:T(8,128)(2,1)S(1)}, bf16[4,1024,128]{2,1,0:T(8,128)(2,1)}, bf16[512,256]{1,0:T(8,128)(2,1)}, bf16[64,128]{1,0:T(8,128)(2,1)}, bf16[64,128]{1,0:T(8,128)(2,1)}) custom-call(s32[20]{0:T(128)S(1)} %concatenate.7.info, bf16[4,512,128]{2,1,0:T(8,128)(2,1)S(1)} %pad_maximum_fusion.rows_ref.refs_0_, ...), custom_call_target="tpu_custom_call" | custom-call | flops 6039797760 | bytes 7340032 | tf_op jit(solution)/shard_map/row_grads/pallas_call | solution.py:268
  104.3 1.9 %collective-permute-start.7 = (bf16[4,1024,128]{2,1,0:T(8,128)(2,1)}, bf16[4,1024,128]{2,1,0:T(8,128)(2,1)S(1)}, u32[]{:S(2)}, u32[]{:S(2)}) collective-permute-start(bf16[4,1024,128]{2,1,0:T(8,128)(2,1)} %get-tuple-element.14), channel_id=1, source_target_pairs={{0,8},{8,0},{1,9},{9,1},{2,10},{10,2},{3,11},{11,3},{4,12},{12,4},... | collective-permute-start | bytes 3145736 | tf_op jit(solution)/shard_map/ppermute | solution.py:33
  106.3 15.0 %all-to-all-start.2 = ((bf16[64,8,256]{2,1,0:T(8,128)(2,1)}), bf16[64,8,256]{2,1,0:T(8,128)(2,1)S(1)}, u32[]{:S(2)}, u32[]{:S(2)}) async-start(bf16[64,8,256]{2,1,0:T(8,128)(2,1)} %bitcast.20), calls=%async_computation.2 | async-start | bytes 524288 | tf_op jit(solution)/shard_map/all_to_all | solution.py:309
  121.3 0.3 add_convert_fusion
  121.6 3.1 %collective-permute-start.8 = (bf16[1024,128]{1,0:T(8,128)(2,1)S(1)}, bf16[1024,128]{1,0:T(8,128)(2,1)S(1)}, u32[]{:S(2)}, u32[]{:S(2)}) collective-permute-start(bf16[1024,128]{1,0:T(8,128)(2,1)S(1)} %get-tuple-element.22), channel_id=1, source_target_pairs={{0,48},{16,0},{32,16},{48,32},{1,49},{17,1},{33,17},{49,33},{2,50}... | collective-permute-start | bytes 786440 | tf_op jit(solution)/shard_map/ppermute | solution.py:33
  124.7 2.7 %collective-permute-start.10 = (bf16[1024,128]{1,0:T(8,128)(2,1)S(1)}, bf16[1024,128]{1,0:T(8,128)(2,1)S(1)}, u32[]{:S(2)}, u32[]{:S(2)}) collective-permute-start(bf16[1024,128]{1,0:T(8,128)(2,1)S(1)} %get-tuple-element.23), channel_id=1, source_target_pairs={{0,16},{16,32},{32,48},{48,0},{1,17},{17,33},{33,49},{49,1},{2,18}... | collective-permute-start | bytes 786440 | tf_op jit(solution)/shard_map/ppermute | solution.py:33
  127.5 2.6 %collective-permute-start.9 = (bf16[1024,128]{1,0:T(8,128)(2,1)S(1)}, bf16[1024,128]{1,0:T(8,128)(2,1)S(1)}, u32[]{:S(2)}, u32[]{:S(2)}) collective-permute-start(bf16[1024,128]{1,0:T(8,128)(2,1)S(1)} %get-tuple-element.24), channel_id=1, source_target_pairs={{0,32},{16,48},{32,0},{48,16},{1,33},{17,49},{33,1},{49,17},{2,34}... | collective-permute-start | bytes 786440 | tf_op jit(solution)/shard_map/ppermute | solution.py:33
  130.0 14.4 %all-to-all-done.2 = bf16[64,8,256]{2,1,0:T(8,128)(2,1)S(1)} async-done(((bf16[64,8,256]{2,1,0:T(8,128)(2,1)}), bf16[64,8,256]{2,1,0:T(8,128)(2,1)S(1)}, u32[]{:S(2)}, u32[]{:S(2)}) %all-to-all-start.2) | async-done | bytes 262176 | tf_op jit(solution)/shard_map/all_to_all | solution.py:309
  144.5 0.7 copy-done.8
  145.1 1.7 %sum_planes.1 = (bf16[8,8,128]{2,1,0:T(8,128)(2,1)}, bf16[8,8,128]{2,1,0:T(8,128)(2,1)}) custom-call(bf16[8,8,8,256]{3,2,1,0:T(8,128)(2,1)} %bitcast.53), custom_call_target="tpu_custom_call" | custom-call | tf_op jit(solution)/shard_map/sum_planes/pallas_call | solution.py:289
  146.9 0.8 fusion.7
  (39 shorter events, 0.4 us)
Async XLA Ops:
  0.6 20.0 %copy-start.9 = (bf16[64,8,128]{2,1,0:T(8,128)(2,1)S(1)}, bf16[64,8,128]{2,1,0:T(8,128)(2,1)}, u32[]{:S(2)}) copy-start(bf16[64,8,128]{2,1,0:T(8,128)(2,1)} %param.17) | copy-start | bytes 393220
  0.6 20.0 %copy-start.11 = (bf16[64,8,128]{2,1,0:T(8,128)(2,1)S(1)}, bf16[64,8,128]{2,1,0:T(8,128)(2,1)}, u32[]{:S(2)}) copy-start(bf16[64,8,128]{2,1,0:T(8,128)(2,1)} %param.14) | copy-start | bytes 393220
  0.7 20.0 %copy-start.10 = (bf16[64,8,128]{2,1,0:T(8,128)(2,1)S(1)}, bf16[64,8,128]{2,1,0:T(8,128)(2,1)}, u32[]{:S(2)}) copy-start(bf16[64,8,128]{2,1,0:T(8,128)(2,1)} %param.13) | copy-start | bytes 393220
  0.7 20.0 %copy-start.12 = (bf16[64,8,128]{2,1,0:T(8,128)(2,1)S(1)}, bf16[64,8,128]{2,1,0:T(8,128)(2,1)}, u32[]{:S(2)}) copy-start(bf16[64,8,128]{2,1,0:T(8,128)(2,1)} %param.10) | copy-start | bytes 393220
  0.7 32.9 %copy-start.13 = (s32[16]{0:T(128)S(1)}, s32[16]{0:T(128)}, u32[]{:S(2)}) copy-start(s32[16]{0:T(128)} %param.19) | copy-start | bytes 196
  0.7 54.2 %copy-start = (bf16[64,1,128]{2,0,1:T(8,128)(2,1)S(1)}, bf16[64,1,128]{2,0,1:T(8,128)(2,1)}, u32[]{:S(2)}) copy-start(bf16[64,1,128]{2,0,1:T(8,128)(2,1)} %param.15) | copy-start | bytes 49156
  0.7 54.2 %copy-start.7 = (bf16[64,1,128]{2,0,1:T(8,128)(2,1)S(1)}, bf16[64,1,128]{2,0,1:T(8,128)(2,1)}, u32[]{:S(2)}) copy-start(bf16[64,1,128]{2,0,1:T(8,128)(2,1)} %param.16) | copy-start | bytes 49156
  2.3 52.6 %all-to-all-start = ((bf16[64,8,256]{2,1,0:T(8,128)(2,1)}), bf16[64,8,256]{2,1,0:T(8,128)(2,1)S(1)}, u32[]{:S(2)}, u32[]{:S(2)}) async-start(bf16[64,8,256]{2,1,0:T(8,128)(2,1)} %bitcast.8), calls=%async_computation | async-start | bytes 524288 | tf_op jit(solution)/shard_map/all_to_all | solution.py:298
  20.8 26.5 %collective-permute-start.2 = (bf16[4,512,128]{2,1,0:T(8,128)(2,1)S(1)}, bf16[4,512,128]{2,1,0:T(8,128)(2,1)S(1)}, u32[]{:S(2)}, u32[]{:S(2)}) collective-permute-start(bf16[4,512,128]{2,1,0:T(8,128)(2,1)S(1)} %pad_maximum_fusion.rows_ref.refs_0_), channel_id=1, source_target_pairs={{0,48},{16,0},{32,16},{48,32},{1,49},{17,1},{33,17},{49,33},{2,50}... | collective-permute-start | bytes 1572872 | tf_op jit(solution)/shard_map/ppermute | solution.py:33
  25.5 23.8 %collective-permute-start.1 = (bf16[4,512,128]{2,1,0:T(8,128)(2,1)S(1)}, bf16[4,512,128]{2,1,0:T(8,128)(2,1)S(1)}, u32[]{:S(2)}, u32[]{:S(2)}) collective-permute-start(bf16[4,512,128]{2,1,0:T(8,128)(2,1)S(1)} %pad_maximum_fusion.rows_ref.refs_0_), channel_id=1, source_target_pairs={{0,32},{16,48},{32,0},{48,16},{1,33},{17,49},{33,1},{49,17},{2,34}... | collective-permute-start | bytes 1572872 | tf_op jit(solution)/shard_map/ppermute | solution.py:33
  28.2 24.7 %collective-permute-start = (bf16[4,512,128]{2,1,0:T(8,128)(2,1)S(1)}, bf16[4,512,128]{2,1,0:T(8,128)(2,1)S(1)}, u32[]{:S(2)}, u32[]{:S(2)}) collective-permute-start(bf16[4,512,128]{2,1,0:T(8,128)(2,1)S(1)} %pad_maximum_fusion.rows_ref.refs_0_), channel_id=1, source_target_pairs={{0,16},{16,32},{32,48},{48,0},{1,17},{17,33},{33,49},{49,1},{2,18}... | collective-permute-start | bytes 1572872 | tf_op jit(solution)/shard_map/ppermute | solution.py:33
  31.0 25.8 %collective-permute-start.3 = (bf16[4,512,128]{2,1,0:T(8,128)(2,1)S(1)}, bf16[4,512,128]{2,1,0:T(8,128)(2,1)S(1)}, u32[]{:S(2)}, u32[]{:S(2)}) collective-permute-start(bf16[4,512,128]{2,1,0:T(8,128)(2,1)S(1)} %pad_maximum_fusion.rows_ref.refs_0_), channel_id=1, source_target_pairs={{0,8},{8,0},{1,9},{9,1},{2,10},{10,2},{3,11},{11,3},{4,12},{12,4},... | collective-permute-start | bytes 1572872 | tf_op jit(solution)/shard_map/ppermute | solution.py:33
  47.3 9.4 %collective-permute-start.6 = (bf16[4,512,128]{2,1,0:T(8,128)(2,1)S(1)}, bf16[4,512,128]{2,1,0:T(8,128)(2,1)}, u32[]{:S(2)}, u32[]{:S(2)}) collective-permute-start(bf16[4,512,128]{2,1,0:T(8,128)(2,1)S(1)} %collective-permute-done.2.refs_2_.refs_3_), channel_id=1, source_target_pairs={{0,8},{8,0},{1,9},{9,1},{2,10},{10,2},{3,11},{11,3},{4,12},{12,4},... | collective-permute-start | bytes 1572872 | tf_op jit(solution)/shard_map/ppermute | solution.py:33
  49.3 7.6 %copy-start.1 = (bf16[4,512,128]{2,1,0:T(8,128)(2,1)}, bf16[4,512,128]{2,1,0:T(8,128)(2,1)S(1)}, u32[]{:S(2)}) copy-start(bf16[4,512,128]{2,1,0:T(8,128)(2,1)S(1)} %collective-permute-done.1.refs_1_.refs_2_) | copy-start | bytes 1572868
  49.3 7.5 %collective-permute-start.5 = (bf16[4,512,128]{2,1,0:T(8,128)(2,1)S(1)}, bf16[4,512,128]{2,1,0:T(8,128)(2,1)}, u32[]{:S(2)}, u32[]{:S(2)}) collective-permute-start(bf16[4,512,128]{2,1,0:T(8,128)(2,1)S(1)} %collective-permute-done.1.refs_1_.refs_2_), channel_id=1, source_target_pairs={{0,8},{8,0},{1,9},{9,1},{2,10},{10,2},{3,11},{11,3},{4,12},{12,4},... | collective-permute-start | bytes 1572872 | tf_op jit(solution)/shard_map/ppermute | solution.py:33
  52.9 3.9 %copy-start.3 = (bf16[4,512,128]{2,1,0:T(8,128)(2,1)}, bf16[4,512,128]{2,1,0:T(8,128)(2,1)S(1)}, u32[]{:S(2)}) copy-start(bf16[4,512,128]{2,1,0:T(8,128)(2,1)S(1)} %collective-permute-done.refs_0_.refs_1_) | copy-start | bytes 1572868
  52.9 3.9 %collective-permute-start.4 = (bf16[4,512,128]{2,1,0:T(8,128)(2,1)S(1)}, bf16[4,512,128]{2,1,0:T(8,128)(2,1)}, u32[]{:S(2)}, u32[]{:S(2)}) collective-permute-start(bf16[4,512,128]{2,1,0:T(8,128)(2,1)S(1)} %collective-permute-done.refs_0_.refs_1_), channel_id=1, source_target_pairs={{0,8},{8,0},{1,9},{9,1},{2,10},{10,2},{3,11},{11,3},{4,12},{12,4},... | collective-permute-start | bytes 1572872 | tf_op jit(solution)/shard_map/ppermute | solution.py:33
  56.7 10.1 %copy-start.5 = (bf16[4,512,128]{2,1,0:T(8,128)(2,1)}, bf16[4,512,128]{2,1,0:T(8,128)(2,1)S(1)}, u32[]{:S(2)}) copy-start(bf16[4,512,128]{2,1,0:T(8,128)(2,1)S(1)} %collective-permute-done.3.refs_3_.refs_4_) | copy-start | bytes 1572868
  66.9 14.1 %all-to-all-start.1 = ((f32[8,8,4,512]{3,2,1,0:T(4,128)}), f32[8,8,4,512]{3,2,1,0:T(4,128)S(1)}, u32[]{:S(2)}, u32[]{:S(2)}) async-start(f32[8,8,4,512]{3,2,1,0:T(4,128)} %row_stats.1), calls=%async_computation.1 | async-start | bytes 1048576 | tf_op jit(solution)/shard_map/all_to_all | solution.py:306
  81.0 1.0 copy-start.2
  82.1 1.0 copy-start.4
  83.1 1.0 copy-start.6
  104.3 16.9 %collective-permute-start.7 = (bf16[4,1024,128]{2,1,0:T(8,128)(2,1)}, bf16[4,1024,128]{2,1,0:T(8,128)(2,1)S(1)}, u32[]{:S(2)}, u32[]{:S(2)}) collective-permute-start(bf16[4,1024,128]{2,1,0:T(8,128)(2,1)} %get-tuple-element.14), channel_id=1, source_target_pairs={{0,8},{8,0},{1,9},{9,1},{2,10},{10,2},{3,11},{11,3},{4,12},{12,4},... | collective-permute-start | bytes 3145736 | tf_op jit(solution)/shard_map/ppermute | solution.py:33
  106.3 38.2 %all-to-all-start.2 = ((bf16[64,8,256]{2,1,0:T(8,128)(2,1)}), bf16[64,8,256]{2,1,0:T(8,128)(2,1)S(1)}, u32[]{:S(2)}, u32[]{:S(2)}) async-start(bf16[64,8,256]{2,1,0:T(8,128)(2,1)} %bitcast.20), calls=%async_computation.2 | async-start | bytes 524288 | tf_op jit(solution)/shard_map/all_to_all | solution.py:309
  121.6 25.2 %collective-permute-start.8 = (bf16[1024,128]{1,0:T(8,128)(2,1)S(1)}, bf16[1024,128]{1,0:T(8,128)(2,1)S(1)}, u32[]{:S(2)}, u32[]{:S(2)}) collective-permute-start(bf16[1024,128]{1,0:T(8,128)(2,1)S(1)} %get-tuple-element.22), channel_id=1, source_target_pairs={{0,48},{16,0},{32,16},{48,32},{1,49},{17,1},{33,17},{49,33},{2,50}... | collective-permute-start | bytes 786440 | tf_op jit(solution)/shard_map/ppermute | solution.py:33
  124.7 22.1 %collective-permute-start.10 = (bf16[1024,128]{1,0:T(8,128)(2,1)S(1)}, bf16[1024,128]{1,0:T(8,128)(2,1)S(1)}, u32[]{:S(2)}, u32[]{:S(2)}) collective-permute-start(bf16[1024,128]{1,0:T(8,128)(2,1)S(1)} %get-tuple-element.23), channel_id=1, source_target_pairs={{0,16},{16,32},{32,48},{48,0},{1,17},{17,33},{33,49},{49,1},{2,18}... | collective-permute-start | bytes 786440 | tf_op jit(solution)/shard_map/ppermute | solution.py:33
  127.5 19.4 %collective-permute-start.9 = (bf16[1024,128]{1,0:T(8,128)(2,1)S(1)}, bf16[1024,128]{1,0:T(8,128)(2,1)S(1)}, u32[]{:S(2)}, u32[]{:S(2)}) collective-permute-start(bf16[1024,128]{1,0:T(8,128)(2,1)S(1)} %get-tuple-element.24), channel_id=1, source_target_pairs={{0,32},{16,48},{32,0},{48,16},{1,33},{17,49},{33,1},{49,17},{2,34}... | collective-permute-start | bytes 786440 | tf_op jit(solution)/shard_map/ppermute | solution.py:33
  144.5 0.7 copy-start.8

commit v3 on v2

v3 whole, which is shorter than its diff:
```python
import math

import jax
import jax.numpy as jnp
from jax import lax
from jax.experimental import pallas as pl
from jax.experimental.pallas import tpu as pltpu
from jax.sharding import Mesh, PartitionSpec as P

AXES = (("zl", 8), ("x", 4), ("core", 2), ("zh", 2), ("y", 4))
CTX = ("zl", "x", "core")
GRP = ("zh", "y")
FAR = ("zl", "zh", "y")
NEAR = ("x", "core")
X, CORES, ZL = 4, 2, 8
BLOCKS = X * CORES

HD = 128
TOKENS = 64
ROWS = 512
KEYS = ZL * TOKENS
MASKED = -1e30
SCALING = 1.0 / math.sqrt(HD)
LOG2E = math.log2(math.e)
SCALE2 = SCALING * LOG2E
F32 = jnp.float32
BF16 = jnp.bfloat16
NT = (((1,), (1,)), ((), ()))


def shifted(value, axis, steps):
    count = lax.axis_size(axis)
    return lax.ppermute(value, axis, [(i, (i + steps) % count) for i in range(count)])


def owner(block, info):
    return (info[0] + X - block % X) % X, (info[1] + block // X) % CORES


def first_tokens(block, kind, info):
    owner_x, owner_core = owner(block, info)
    if kind == 0:
        return ((info[2] * X + owner_x) * CORES + owner_core) * TOKENS, info[3]
    return ((owner_x % 2) * CORES + owner_core) * TOKENS, info[4 + info[2] * 2 + owner_x // 2]


def row_tokens():
    return lax.broadcasted_iota(jnp.int32, (1, ROWS), 1) // 8


def prompt_scores(block, kind, info, keys, queries):
    scores = lax.dot_general(keys, queries, NT, preferred_element_type=F32) * SCALE2
    key = lax.broadcasted_iota(jnp.int32, (KEYS, 1), 0)
    key_pos = (key // TOKENS) * (BLOCKS * TOKENS) + key % TOKENS + (info[0] * CORES + info[1]) * TOKENS
    if kind == 1:
        limit = jnp.zeros((1, ROWS), jnp.int32) + (info[3] - 1)
    else:
        limit = first_tokens(block, 0, info)[0] + row_tokens()
    return jnp.where(key_pos <= limit, scores, MASKED)


def roll_scores(block, info, keys, queries):
    scores = lax.dot_general(keys, queries, NT, preferred_element_type=F32) * SCALE2
    key_pos = lax.broadcasted_iota(jnp.int32, (TOKENS, 1), 0) + ((info[0] % 2) * CORES + info[1]) * TOKENS
    return jnp.where(key_pos <= first_tokens(block, 1, info)[0] + row_tokens(), scores, MASKED)


def partial_stats(scores, weight_grad):
    top = jnp.max(scores, axis=0, keepdims=True)
    weights = jnp.exp2(scores - top)
    total = jnp.sum(weights, axis=0, keepdims=True)
    product = jnp.sum(weights * weight_grad, axis=0, keepdims=True)
    return top + jnp.log2(total), product / total


def merged(first, second):
    (log_a, delta_a), (log_b, delta_b) = first, second
    top = jnp.maximum(log_a, log_b)
    share_a, share_b = jnp.exp2(log_a - top), jnp.exp2(log_b - top)
    total = share_a + share_b
    return top + jnp.log2(total), (delta_a * share_a + delta_b * share_b) / total


def fetch(refs, rows_s, sems):
    for i, ref in enumerate(refs):
        pltpu.make_async_copy(ref, rows_s.at[i], sems.at[i]).start()


def arrive(i, refs, rows_s, sems):
    pltpu.make_async_copy(refs[0], rows_s.at[i], sems.at[i]).wait()


def sees_roll(block, info):
    return owner(block, info)[0] // 2 == info[0] // 2


def stats_kernel(info, *refs):
    rows, (kv_ref, rkv_ref, out_ref, all_ref, rows_s, stats_s, sems, out_sems) = refs[:BLOCKS], refs[BLOCKS:]
    fetch(rows, rows_s, sems)

    def keep(block):
        return pltpu.make_async_copy(rows_s.at[block], all_ref.at[block], out_sems.at[block])

    @pl.loop(0, BLOCKS)
    def _(block):
        arrive(block, rows, rows_s, sems)
        keep(block).start()
        owner_x, owner_core = owner(block, info)
        at = owner_x * CORES + owner_core

        def put(kind, stats):
            stats_s[at, 2 * kind : 2 * kind + 1, :] = stats[0]
            stats_s[at, 2 * kind + 1 : 2 * kind + 2, :] = stats[1]

        for kind in (0, 1):
            queries, grads = rows_s[block, kind], rows_s[block, 2 + kind]
            scores = prompt_scores(block, kind, info, kv_ref[:, :HD], queries)
            weight_grad = lax.dot_general(kv_ref[:, HD:], grads, NT, preferred_element_type=F32)
            put(kind, partial_stats(scores, weight_grad))

        @pl.when(sees_roll(block, info))
        def _():
            roll = roll_scores(block, info, rkv_ref[:, :HD], rows_s[block, 1])
            roll_grad = lax.dot_general(rkv_ref[:, HD:], rows_s[block, 3], NT, preferred_element_type=F32)
            put(1, merged((stats_s[at, 2:3, :], stats_s[at, 3:4, :]), partial_stats(roll, roll_grad)))

    for peer in range(BLOCKS):
        out_ref[peer] = stats_s[...]
    for block in range(BLOCKS):
        keep(block).wait()


def combined(stats_ref, block, kind, info):
    owner_x, owner_core = owner(block, info)
    at = owner_x * CORES + owner_core
    logs, deltas = stats_ref[:, at, 2 * kind, :], stats_ref[:, at, 2 * kind + 1, :]
    top = jnp.max(logs, axis=0, keepdims=True)
    shares = jnp.exp2(logs - top)
    total = jnp.sum(shares, axis=0, keepdims=True)
    start, length = first_tokens(block, kind, info)
    log_total = jnp.where(start + row_tokens() < length, top + jnp.log2(total), -MASKED)
    return log_total, jnp.sum(shares * deltas, axis=0, keepdims=True) / total


def block_grads(scores, weight_grad, log_total, delta, queries, grads, keys_t):
    weights = jnp.exp2(scores - log_total)
    score_grad = (weights * (weight_grad - delta)).astype(BF16)
    key_part = jnp.dot(score_grad, queries, preferred_element_type=F32)
    value_part = jnp.dot(weights.astype(BF16), grads, preferred_element_type=F32)
    query_t = jnp.dot(keys_t, score_grad, preferred_element_type=F32)
    return query_t, key_part, value_part


def grads_kernel(info, rows_ref, stats_ref, kv_ref, kt_ref, rkv_ref, rkt_ref, *refs):
    (dq0_ref, dq1_ref, dkv_ref, drk_ref, drv_ref, rows_s, dqt_s, acc, roll_acc, sems) = refs
    rows = [rows_ref.at[block] for block in range(BLOCKS)]
    fetch(rows, rows_s, sems)
    acc[...] = jnp.zeros_like(acc)
    roll_acc[...] = jnp.zeros_like(roll_acc)

    @pl.loop(0, BLOCKS)
    def _(block):
        arrive(block, rows, rows_s, sems)
        for kind in (0, 1):
            log_total, delta = combined(stats_ref, block, kind, info)
            queries, grads = rows_s[block, kind], rows_s[block, 2 + kind]
            scores = prompt_scores(block, kind, info, kv_ref[:, :HD], queries)
            weight_grad = lax.dot_general(kv_ref[:, HD:], grads, NT, preferred_element_type=F32)
            query_t, key_part, value_part = block_grads(
                scores, weight_grad, log_total, delta, queries, grads, kt_ref[...]
            )
            dqt_s[kind] = query_t
            acc[:, :HD] += key_part
            acc[:, HD:] += value_part

        @pl.when(sees_roll(block, info))
        def _():
            log_total, delta = combined(stats_ref, block, 1, info)
            queries, grads = rows_s[block, 1], rows_s[block, 3]
            roll = roll_scores(block, info, rkv_ref[:, :HD], queries)
            roll_grad = lax.dot_general(rkv_ref[:, HD:], grads, NT, preferred_element_type=F32)
            query_r, key_r, value_r = block_grads(roll, roll_grad, log_total, delta, queries, grads, rkt_ref[...])
            dqt_s[1] += query_r
            roll_acc[:, :HD] += key_r
            roll_acc[:, HD:] += value_r

        for kind in (0, 1):
            out = (dqt_s[kind] * SCALING).T.astype(BF16)
            at = slice(kind * ROWS, kind * ROWS + ROWS)

            @pl.when(block < X)
            def _():
                dq0_ref[block, at, :] = out

            @pl.when(block >= X)
            def _():
                dq1_ref[block - X, at, :] = out

    dkv_ref[:, :HD] = (acc[:, :HD] * SCALING).astype(BF16)
    dkv_ref[:, HD:] = acc[:, HD:].astype(BF16)
    drk_ref[...] = (roll_acc[:, :HD] * SCALING).astype(BF16)
    drv_ref[...] = roll_acc[:, HD:].astype(BF16)


def finish_kernel(back_ref, dk_ref, dv_ref):
    total = jnp.sum(back_ref[...].astype(F32), axis=0)
    for head in range(total.shape[0]):
        dk_ref[:, head, :] = total[head, :, :HD].astype(BF16)
        dv_ref[:, head, :] = total[head, :, HD:].astype(BF16)


VMEM = pl.BlockSpec(memory_space=pltpu.VMEM)
SMEM = pl.BlockSpec(memory_space=pltpu.SMEM)
HBM = pl.BlockSpec(memory_space=pltpu.HBM)
PARAMS = pltpu.CompilerParams(vmem_limit_bytes=52 * 2**20)
COST = 2 * 1024 * 576 * HD


WAIT_FLOPS = 100 * 10**9


def cost(flops, byte_count):
    return pl.CostEstimate(flops=flops, bytes_accessed=byte_count, transcendentals=0)


def call_stats(info, rows, kv, rkv):
    return pl.pallas_call(
        stats_kernel,
        out_shape=(
            jax.ShapeDtypeStruct((BLOCKS, BLOCKS, 4, ROWS), F32),
            jax.ShapeDtypeStruct((BLOCKS, 4, ROWS, HD), BF16),
        ),
        in_specs=[SMEM] + [HBM] * BLOCKS + [VMEM] * 2,
        out_specs=(VMEM, HBM),
        scratch_shapes=[
            pltpu.VMEM((BLOCKS, 4, ROWS, HD), BF16),
            pltpu.VMEM((BLOCKS, 4, ROWS), F32),
            pltpu.SemaphoreType.DMA((BLOCKS,)),
            pltpu.SemaphoreType.DMA((BLOCKS,)),
        ],
        compiler_params=PARAMS,
        cost_estimate=cost(2 * 8 * COST, 5 * 2**20),
        name="row_stats",
    )(info, *rows, kv, rkv)


def call_grads(info, rows, stats, kv, kt, rkv, rkt):
    half = jax.ShapeDtypeStruct((X, 2 * ROWS, HD), BF16)
    roll = jax.ShapeDtypeStruct((TOKENS, HD), BF16)
    return pl.pallas_call(
        grads_kernel,
        out_shape=(half, half, jax.ShapeDtypeStruct((KEYS, 2 * HD), BF16), roll, roll),
        in_specs=[SMEM, HBM] + [VMEM] * 5,
        out_specs=(VMEM,) * 5,
        scratch_shapes=[
            pltpu.VMEM((BLOCKS, 4, ROWS, HD), BF16),
            pltpu.VMEM((2, HD, ROWS), F32),
            pltpu.VMEM((KEYS, 2 * HD), F32),
            pltpu.VMEM((TOKENS, 2 * HD), F32),
            pltpu.SemaphoreType.DMA((BLOCKS,)),
        ],
        compiler_params=PARAMS,
        cost_estimate=cost(5 * 8 * COST, 7 * 2**20),
        name="row_grads",
    )(info, rows, stats, kv, kt, rkv, rkt)


def call_finish(back):
    tokens, heads = back.shape[2], back.shape[1]
    out = jax.ShapeDtypeStruct((tokens, heads, HD), BF16)
    return pl.pallas_call(
        finish_kernel,
        out_shape=(out, out),
        in_specs=[VMEM],
        out_specs=(VMEM, VMEM),
        compiler_params=pltpu.CompilerParams(vmem_limit_bytes=4 * 2**20),
        cost_estimate=cost(WAIT_FLOPS, 2**18),
        name="sum_planes",
    )(back)


def per_device(q_prompt, k_prompt, v_prompt, grad_prompt, q_roll, k_roll, v_roll, grad_roll, prompt_len, roll_len):
    zl, x, core = (lax.axis_index(name) for name in CTX)
    pair = jnp.transpose(jnp.concatenate([k_prompt, v_prompt], axis=-1), (1, 0, 2))
    sent = jnp.broadcast_to(pair[None], (ZL,) + pair.shape).reshape(ZL * pair.shape[0], *pair.shape[1:])
    kv = lax.all_to_all(sent, FAR, split_axis=0, concat_axis=0, tiled=True).reshape(KEYS, 2 * HD)
    own = jnp.stack([q_prompt, q_roll, grad_prompt, grad_roll]).reshape(4, ROWS, HD)
    rows = [own] + [shifted(own, "x", steps) for steps in range(1, X)]
    rows = rows + [shifted(r, "core", 1) for r in rows]
    rkv = jnp.concatenate([k_roll, v_roll], axis=-1).reshape(TOKENS, 2 * HD)
    info = jnp.concatenate([jnp.stack([x, core, zl]).astype(jnp.int32), prompt_len, roll_len])
    stats, rows = call_stats(info, rows, kv, rkv)
    stats = lax.all_to_all(stats, NEAR, split_axis=0, concat_axis=0, tiled=True)
    dq_same, dq_other, dkv, drk, drv = call_grads(info, rows, stats, kv, kv[:, :HD].T, rkv, rkv[:, :HD].T)
    groups = k_prompt.shape[1]
    back = lax.all_to_all(
        dkv.reshape(ZL * groups, TOKENS // groups, 2 * HD), FAR, split_axis=0, concat_axis=0, tiled=True
    )
    dk_prompt, dv_prompt = call_finish(back.reshape(ZL, groups, TOKENS // groups, 2 * HD))
    arrived = shifted(dq_other, "core", 1)
    halves = (dq_same.astype(F32) + arrived.astype(F32)).astype(BF16)
    parts = [halves[0]] + [shifted(halves[steps], "x", -steps) for steps in range(1, X)]
    dq = [
        sum(part[first : first + ROWS].astype(F32) for part in parts).astype(BF16).reshape(q_prompt.shape)
        for first in (0, ROWS)
    ]
    return (dq[0], dk_prompt, dv_prompt, dq[1], drk.reshape(k_roll.shape), drv.reshape(v_roll.shape))


def solution(mesh):
    names = tuple(name for name, _ in AXES)
    fine = Mesh(mesh.devices.reshape([size for _, size in AXES]), names)
    by_head, by_token = P(CTX, GRP, None), P(CTX + GRP, None, None)
    return jax.shard_map(
        per_device,
        mesh=fine,
        in_specs=(by_head, by_token, by_token, by_head, by_head, by_head, by_head, by_head, P(), P()),
        out_specs=(by_head, by_token, by_token, by_head, by_head, by_head),
        check_vma=False,
    )
```

time: 149 us -> 130 us (0.87)
  starting transfers between devices: 65.8 us -> 58.2 us
  waiting for transfers between devices: 39.5 us -> 33.1 us
  Pallas kernels: 33.7 us -> 29.2 us
  other arithmetic: 2.02 us -> 4.27 us
  local copies, waits for them, and re-layouts: 4.96 us -> 2.77 us
    ppermute x11, waiting for transfers between devices: 15 us -> 0.03 us  [shifted(): lax.ppermute(value, axis, [(i, (i + steps) % count) for i in range(count)])]
    all_to_all x1, waiting for transfers between devices: 0.01 us -> 10.4 us  [per_device(): lax.all_to_all(sent, FAR, split_axis=0, concat_axis=0, tiled=True)]
    all_to_all x1, starting transfers between devices: 15 us -> 5.37 us  [per_device(): lax.all_to_all(dkv.reshape(ZL * groups, TOKENS // groups, 2 * HD), FAR, s...]
    unnamed x30 -> x11, local copies, waits for them, and re-layouts: 4.08 us -> 1.79 us
    ppermute x11, starting transfers between devices: 28.6 us -> 30.9 us  [shifted(): lax.ppermute(value, axis, [(i, (i + steps) % count) for i in range(count)])]
    pallas_call x2 -> x1, Pallas kernels: 11.9 us -> 9.96 us  [call_stats(): pl.pallas_call(stats_kernel, out_shape=(jax.ShapeDtypeStruct((BLOCKS, BLO...]
    all_to_all x1, waiting for transfers between devices: 14.4 us -> 12.6 us  [per_device(): lax.all_to_all(dkv.reshape(ZL * groups, TOKENS // groups, 2 * HD), FAR, s...]
    pallas_call x1, Pallas kernels: 20.2 us -> 18.5 us  [call_grads(): pl.pallas_call(grads_kernel, out_shape=(half, half, jax.ShapeDtypeStruct(...]
  transfers between devices with their start and end apart: 14 -> 14, of which waited for: 5 -> 3; matrix products, arithmetic and copies ran while one was open for 0% -> 4% of each run, Pallas kernels for 2% -> 1%
where the time goes in v3:
time: 130 us; the launch traced here: 129 us
  starting transfers between devices  58.2 us (45%)
  waiting for transfers between devices  33.1 us (25%)
  Pallas kernels  29.2 us (22%)
  other arithmetic  4.27 us (3%)
  local copies, waits for them, and re-layouts  2.77 us (2%)
  between operations  1.57 us (1%)
    ppermute x11, starting transfers between devices, shifted(): lax.ppermute(value, axis, [(i, (i + steps) % count) for i in range(count)])  30.9 us
    pallas_call x1, Pallas kernels, call_grads(): pl.pallas_call(grads_kernel, out_shape=(half, half, jax.ShapeDtypeStruct(...  18.5 us
    all_to_all x1, starting transfers between devices, per_device(): lax.all_to_all(sent, FAR, split_axis=0, concat_axis=0, tiled=True)  18.4 us
    all_to_all x1, waiting for transfers between devices, per_device(): lax.all_to_all(dkv.reshape(ZL * groups, TOKENS // groups, 2 * HD), FAR, s...  12.6 us
    all_to_all x1, waiting for transfers between devices, per_device(): lax.all_to_all(sent, FAR, split_axis=0, concat_axis=0, tiled=True)  10.4 us
    all_to_all x1, waiting for transfers between devices, per_device(): stats = lax.all_to_all(stats, NEAR, split_axis=0, concat_axis=0, tiled=True)  10.1 us
    pallas_call x1, Pallas kernels, call_stats(): pl.pallas_call(stats_kernel, out_shape=(jax.ShapeDtypeStruct((BLOCKS, BLO...  9.96 us
    all_to_all x1, starting transfers between devices, per_device(): lax.all_to_all(dkv.reshape(ZL * groups, TOKENS // groups, 2 * HD), FAR, s...  5.37 us
  transfers between devices with their start and end apart: 14, of which 3 were waited for; matrix products, arithmetic and copies ran while one was open for 4% of the time, Pallas kernels for 1%

profile of v3, /device:TPU:32, one launch (start us, length us, event | category | flops | bytes accessed | tf_op | source)
XLA Modules:
  0.0 129.1 jit_solution(4815636750015514276)
XLA Ops:
  0.6 1.2 pad_maximum_fusion.refs_0_
  1.8 3.4 %collective-permute-start = (bf16[4,512,128]{2,1,0:T(8,128)(2,1)S(1)}, bf16[4,512,128]{2,1,0:T(8,128)(2,1)S(1)}, u32[]{:S(2)}, u32[]{:S(2)}) collective-permute-start(bf16[4,512,128]{2,1,0:T(8,128)(2,1)S(1)} %pad_maximum_fusion.refs_0_), channel_id=1, source_target_pairs={{0,16},{16,32},{32,48},{48,0},{1,17},{17,33},{33,49},{49,1},{2,18}... | collective-permute-start | bytes 1572872 | tf_op jit(solution)/shard_map/ppermute | solution.py:33
  5.2 4.6 %collective-permute-start.1 = (bf16[4,512,128]{2,1,0:T(8,128)(2,1)S(1)}, bf16[4,512,128]{2,1,0:T(8,128)(2,1)S(1)}, u32[]{:S(2)}, u32[]{:S(2)}) collective-permute-start(bf16[4,512,128]{2,1,0:T(8,128)(2,1)S(1)} %pad_maximum_fusion.refs_0_), channel_id=1, source_target_pairs={{0,32},{16,48},{32,0},{48,16},{1,33},{17,49},{33,1},{49,17},{2,34}... | collective-permute-start | bytes 1572872 | tf_op jit(solution)/shard_map/ppermute | solution.py:33
  9.9 3.3 %collective-permute-start.2 = (bf16[4,512,128]{2,1,0:T(8,128)(2,1)S(1)}, bf16[4,512,128]{2,1,0:T(8,128)(2,1)S(1)}, u32[]{:S(2)}, u32[]{:S(2)}) collective-permute-start(bf16[4,512,128]{2,1,0:T(8,128)(2,1)S(1)} %pad_maximum_fusion.refs_0_), channel_id=1, source_target_pairs={{0,48},{16,0},{32,16},{48,32},{1,49},{17,1},{33,17},{49,33},{2,50}... | collective-permute-start | bytes 1572872 | tf_op jit(solution)/shard_map/ppermute | solution.py:33
  13.2 0.7 maximum_bitcast_fusion.1
  14.0 0.7 broadcast_in_dim.2
  14.7 18.4 %all-to-all-start = ((bf16[64,8,256]{2,1,0:T(8,128)(2,1)}), bf16[64,8,256]{2,1,0:T(8,128)(2,1)S(1)}, u32[]{:S(2)}, u32[]{:S(2)}) async-start(bf16[64,8,256]{2,1,0:T(8,128)(2,1)} %bitcast.8), calls=%async_computation | async-start | bytes 524288 | tf_op jit(solution)/shard_map/all_to_all | solution.py:286
  33.1 1.9 %collective-permute-start.3 = (bf16[4,512,128]{2,1,0:T(8,128)(2,1)S(1)}, bf16[4,512,128]{2,1,0:T(8,128)(2,1)S(1)}, u32[]{:S(2)}, u32[]{:S(2)}) collective-permute-start(bf16[4,512,128]{2,1,0:T(8,128)(2,1)S(1)} %pad_maximum_fusion.refs_0_), channel_id=1, source_target_pairs={{0,8},{8,0},{1,9},{9,1},{2,10},{10,2},{3,11},{11,3},{4,12},{12,4},... | collective-permute-start | bytes 1572872 | tf_op jit(solution)/shard_map/ppermute | solution.py:33
  35.0 2.4 %collective-permute-start.4 = (bf16[4,512,128]{2,1,0:T(8,128)(2,1)S(1)}, bf16[4,512,128]{2,1,0:T(8,128)(2,1)}, u32[]{:S(2)}, u32[]{:S(2)}) collective-permute-start(bf16[4,512,128]{2,1,0:T(8,128)(2,1)S(1)} %collective-permute-done.refs_1_), channel_id=1, source_target_pairs={{0,8},{8,0},{1,9},{9,1},{2,10},{10,2},{3,11},{11,3},{4,12},{12,4},... | collective-permute-start | bytes 1572872 | tf_op jit(solution)/shard_map/ppermute | solution.py:33
  37.4 0.0 collective-permute-done.1.refs_2_
  37.5 1.9 %collective-permute-start.5 = (bf16[4,512,128]{2,1,0:T(8,128)(2,1)S(1)}, bf16[4,512,128]{2,1,0:T(8,128)(2,1)}, u32[]{:S(2)}, u32[]{:S(2)}) collective-permute-start(bf16[4,512,128]{2,1,0:T(8,128)(2,1)S(1)} %collective-permute-done.1.refs_2_), channel_id=1, source_target_pairs={{0,8},{8,0},{1,9},{9,1},{2,10},{10,2},{3,11},{11,3},{4,12},{12,4},... | collective-permute-start | bytes 1572872 | tf_op jit(solution)/shard_map/ppermute | solution.py:33
  39.4 2.4 %collective-permute-start.6 = (bf16[4,512,128]{2,1,0:T(8,128)(2,1)S(1)}, bf16[4,512,128]{2,1,0:T(8,128)(2,1)}, u32[]{:S(2)}, u32[]{:S(2)}) collective-permute-start(bf16[4,512,128]{2,1,0:T(8,128)(2,1)S(1)} %collective-permute-done.2.refs_3_), channel_id=1, source_target_pairs={{0,8},{8,0},{1,9},{9,1},{2,10},{10,2},{3,11},{11,3},{4,12},{12,4},... | collective-permute-start | bytes 1572872 | tf_op jit(solution)/shard_map/ppermute | solution.py:33
  42.5 0.8 copy.24
  43.3 0.8 copy.25
  44.2 0.1 copy.26.refs_9_.rkv_ref
  44.3 0.1 concatenate.10.info
  44.4 10.4 %all-to-all-done = bf16[64,8,256]{2,1,0:T(8,128)(2,1)S(1)} async-done(((bf16[64,8,256]{2,1,0:T(8,128)(2,1)}), bf16[64,8,256]{2,1,0:T(8,128)(2,1)S(1)}, u32[]{:S(2)}, u32[]{:S(2)}) %all-to-all-start) | async-done | bytes 262176 | tf_op jit(solution)/shard_map/all_to_all | solution.py:286
  54.8 10.0 %row_stats.1 = (f32[8,8,4,512]{3,2,1,0:T(4,128)}, bf16[8,4,512,128]{3,2,1,0:T(8,128)(2,1)}) custom-call(s32[20]{0:T(128)S(1)} %concatenate.10.info, bf16[4,512,128]{2,1,0:T(8,128)(2,1)S(1)} %pad_maximum_fusion.refs_0_, bf16[4,512,128]{2,1,0:T(8,128)(2,1)S(1)} %collective-permute-done.refs_1_, bf16[4,512,128]{2,1,0:T(8,128)(2,1)} %copy-done.1, ...), custom_call_target="tpu_custom_call" | custom-call | flops 2415919104 | bytes 5242880 | tf_op jit(solution)/shard_map/row_stats/pallas_call | solution.py:227
  64.8 3.5 %all-to-all-start.1 = ((f32[8,8,4,512]{3,2,1,0:T(4,128)}), f32[8,8,4,512]{3,2,1,0:T(4,128)S(1)}, u32[]{:S(2)}, u32[]{:S(2)}) async-start(f32[8,8,4,512]{3,2,1,0:T(4,128)} %get-tuple-element.16), calls=%async_computation.1 | async-start | bytes 1048576 | tf_op jit(solution)/shard_map/all_to_all | solution.py:293
  68.3 0.1 copy.29
  68.4 10.1 %all-to-all-done.1.stats_ref = f32[8,8,4,512]{3,2,1,0:T(4,128)S(1)} async-done(((f32[8,8,4,512]{3,2,1,0:T(4,128)}), f32[8,8,4,512]{3,2,1,0:T(4,128)S(1)}, u32[]{:S(2)}, u32[]{:S(2)}) %all-to-all-start.1) | async-done | bytes 524320 | tf_op jit(solution)/shard_map/all_to_all | solution.py:293
  78.5 18.5 %row_grads.1 = (bf16[4,1024,128]{2,1,0:T(8,128)(2,1)}, bf16[4,1024,128]{2,1,0:T(8,128)(2,1)}, bf16[512,256]{1,0:T(8,128)(2,1)}, bf16[64,128]{1,0:T(8,128)(2,1)}, bf16[64,128]{1,0:T(8,128)(2,1)}) custom-call(s32[20]{0:T(128)S(1)} %concatenate.10.info, bf16[8,4,512,128]{3,2,1,0:T(8,128)(2,1)} %get-tuple-element.15.rows_ref, ...), custom_call_target="tpu_custom_call" | custom-call | flops 6039797760 | bytes 7340032 | tf_op jit(solution)/shard_map/row_grads/pallas_call | solution.py:250
  97.0 1.9 %collective-permute-start.7 = (bf16[4,1024,128]{2,1,0:T(8,128)(2,1)}, bf16[4,1024,128]{2,1,0:T(8,128)(2,1)S(1)}, u32[]{:S(2)}, u32[]{:S(2)}) collective-permute-start(bf16[4,1024,128]{2,1,0:T(8,128)(2,1)} %get-tuple-element.18), channel_id=1, source_target_pairs={{0,8},{8,0},{1,9},{9,1},{2,10},{10,2},{3,11},{11,3},{4,12},{12,4},... | collective-permute-start | bytes 3145736 | tf_op jit(solution)/shard_map/ppermute | solution.py:33
  98.9 5.4 %all-to-all-start.2 = ((bf16[64,8,256]{2,1,0:T(8,128)(2,1)}), bf16[64,8,256]{2,1,0:T(8,128)(2,1)S(1)}, u32[]{:S(2)}, u32[]{:S(2)}) async-start(bf16[64,8,256]{2,1,0:T(8,128)(2,1)} %bitcast.18), calls=%async_computation.2 | async-start | bytes 524288 | tf_op jit(solution)/shard_map/all_to_all | solution.py:296
  104.3 1.5 %add_convert_fusion = bf16[4,1024,128]{2,1,0:T(8,128)(2,1)S(1)} fusion(bf16[4,1024,128]{2,1,0:T(8,128)(2,1)S(1)} %collective-permute-done.7, bf16[4,1024,128]{2,1,0:T(8,128)(2,1)} %get-tuple-element.17), kind=kLoop, calls=%fused_computation | loop fusion | flops 2097152 | bytes 3145728 | tf_op jit(solution)/shard_map/convert_element_type | solution.py:301
  105.8 0.1 slice_bitcast_fusion.2
  105.9 2.5 %collective-permute-start.10 = (bf16[1024,128]{1,0:T(8,128)(2,1)S(1)}, bf16[1024,128]{1,0:T(8,128)(2,1)S(1)}, u32[]{:S(2)}, u32[]{:S(2)}) collective-permute-start(bf16[1024,128]{1,0:T(8,128)(2,1)S(1)} %get-tuple-element.27), channel_id=1, source_target_pairs={{0,16},{16,32},{32,48},{48,0},{1,17},{17,33},{33,49},{49,1},{2,18}... | collective-permute-start | bytes 786440 | tf_op jit(solution)/shard_map/ppermute | solution.py:33
  108.4 4.6 %collective-permute-start.8 = (bf16[1024,128]{1,0:T(8,128)(2,1)S(1)}, bf16[1024,128]{1,0:T(8,128)(2,1)S(1)}, u32[]{:S(2)}, u32[]{:S(2)}) collective-permute-start(bf16[1024,128]{1,0:T(8,128)(2,1)S(1)} %get-tuple-element.26), channel_id=1, source_target_pairs={{0,48},{16,0},{32,16},{48,32},{1,49},{17,1},{33,17},{49,33},{2,50}... | collective-permute-start | bytes 786440 | tf_op jit(solution)/shard_map/ppermute | solution.py:33
  112.9 1.9 %collective-permute-start.9 = (bf16[1024,128]{1,0:T(8,128)(2,1)S(1)}, bf16[1024,128]{1,0:T(8,128)(2,1)S(1)}, u32[]{:S(2)}, u32[]{:S(2)}) collective-permute-start(bf16[1024,128]{1,0:T(8,128)(2,1)S(1)} %get-tuple-element.28), channel_id=1, source_target_pairs={{0,32},{16,48},{32,0},{48,16},{1,33},{17,49},{33,1},{49,17},{2,34}... | collective-permute-start | bytes 786440 | tf_op jit(solution)/shard_map/ppermute | solution.py:33
  114.9 12.6 %all-to-all-done.2 = bf16[64,8,256]{2,1,0:T(8,128)(2,1)S(1)} async-done(((bf16[64,8,256]{2,1,0:T(8,128)(2,1)}), bf16[64,8,256]{2,1,0:T(8,128)(2,1)S(1)}, u32[]{:S(2)}, u32[]{:S(2)}) %all-to-all-start.2) | async-done | bytes 262176 | tf_op jit(solution)/shard_map/all_to_all | solution.py:296
  127.5 0.7 sum_planes.1
  128.3 0.8 fusion.7
  (22 shorter events, 0.1 us)
Async XLA Ops:
  0.6 43.6 %copy-start = (s32[16]{0:T(128)S(1)}, s32[16]{0:T(128)}, u32[]{:S(2)}) copy-start(s32[16]{0:T(128)} %param.19) | copy-start | bytes 196
  1.8 33.2 %collective-permute-start = (bf16[4,512,128]{2,1,0:T(8,128)(2,1)S(1)}, bf16[4,512,128]{2,1,0:T(8,128)(2,1)S(1)}, u32[]{:S(2)}, u32[]{:S(2)}) collective-permute-start(bf16[4,512,128]{2,1,0:T(8,128)(2,1)S(1)} %pad_maximum_fusion.refs_0_), channel_id=1, source_target_pairs={{0,16},{16,32},{32,48},{48,0},{1,17},{17,33},{33,49},{49,1},{2,18}... | collective-permute-start | bytes 1572872 | tf_op jit(solution)/shard_map/ppermute | solution.py:33
  5.2 32.2 %collective-permute-start.1 = (bf16[4,512,128]{2,1,0:T(8,128)(2,1)S(1)}, bf16[4,512,128]{2,1,0:T(8,128)(2,1)S(1)}, u32[]{:S(2)}, u32[]{:S(2)}) collective-permute-start(bf16[4,512,128]{2,1,0:T(8,128)(2,1)S(1)} %pad_maximum_fusion.refs_0_), channel_id=1, source_target_pairs={{0,32},{16,48},{32,0},{48,16},{1,33},{17,49},{33,1},{49,17},{2,34}... | collective-permute-start | bytes 1572872 | tf_op jit(solution)/shard_map/ppermute | solution.py:33
  9.9 29.5 %collective-permute-start.2 = (bf16[4,512,128]{2,1,0:T(8,128)(2,1)S(1)}, bf16[4,512,128]{2,1,0:T(8,128)(2,1)S(1)}, u32[]{:S(2)}, u32[]{:S(2)}) collective-permute-start(bf16[4,512,128]{2,1,0:T(8,128)(2,1)S(1)} %pad_maximum_fusion.refs_0_), channel_id=1, source_target_pairs={{0,48},{16,0},{32,16},{48,32},{1,49},{17,1},{33,17},{49,33},{2,50}... | collective-permute-start | bytes 1572872 | tf_op jit(solution)/shard_map/ppermute | solution.py:33
  14.7 40.0 %all-to-all-start = ((bf16[64,8,256]{2,1,0:T(8,128)(2,1)}), bf16[64,8,256]{2,1,0:T(8,128)(2,1)S(1)}, u32[]{:S(2)}, u32[]{:S(2)}) async-start(bf16[64,8,256]{2,1,0:T(8,128)(2,1)} %bitcast.8), calls=%async_computation | async-start | bytes 524288 | tf_op jit(solution)/shard_map/all_to_all | solution.py:286
  33.1 11.3 %collective-permute-start.3 = (bf16[4,512,128]{2,1,0:T(8,128)(2,1)S(1)}, bf16[4,512,128]{2,1,0:T(8,128)(2,1)S(1)}, u32[]{:S(2)}, u32[]{:S(2)}) collective-permute-start(bf16[4,512,128]{2,1,0:T(8,128)(2,1)S(1)} %pad_maximum_fusion.refs_0_), channel_id=1, source_target_pairs={{0,8},{8,0},{1,9},{9,1},{2,10},{10,2},{3,11},{11,3},{4,12},{12,4},... | collective-permute-start | bytes 1572872 | tf_op jit(solution)/shard_map/ppermute | solution.py:33
  35.0 19.7 %collective-permute-start.4 = (bf16[4,512,128]{2,1,0:T(8,128)(2,1)S(1)}, bf16[4,512,128]{2,1,0:T(8,128)(2,1)}, u32[]{:S(2)}, u32[]{:S(2)}) collective-permute-start(bf16[4,512,128]{2,1,0:T(8,128)(2,1)S(1)} %collective-permute-done.refs_1_), channel_id=1, source_target_pairs={{0,8},{8,0},{1,9},{9,1},{2,10},{10,2},{3,11},{11,3},{4,12},{12,4},... | collective-permute-start | bytes 1572872 | tf_op jit(solution)/shard_map/ppermute | solution.py:33
  37.5 17.3 %copy-start.1 = (bf16[4,512,128]{2,1,0:T(8,128)(2,1)}, bf16[4,512,128]{2,1,0:T(8,128)(2,1)S(1)}, u32[]{:S(2)}) copy-start(bf16[4,512,128]{2,1,0:T(8,128)(2,1)S(1)} %collective-permute-done.1.refs_2_) | copy-start | bytes 1572868
  37.5 17.3 %collective-permute-start.5 = (bf16[4,512,128]{2,1,0:T(8,128)(2,1)S(1)}, bf16[4,512,128]{2,1,0:T(8,128)(2,1)}, u32[]{:S(2)}, u32[]{:S(2)}) collective-permute-start(bf16[4,512,128]{2,1,0:T(8,128)(2,1)S(1)} %collective-permute-done.1.refs_2_), channel_id=1, source_target_pairs={{0,8},{8,0},{1,9},{9,1},{2,10},{10,2},{3,11},{11,3},{4,12},{12,4},... | collective-permute-start | bytes 1572872 | tf_op jit(solution)/shard_map/ppermute | solution.py:33
  39.4 15.4 %copy-start.2 = (bf16[4,512,128]{2,1,0:T(8,128)(2,1)}, bf16[4,512,128]{2,1,0:T(8,128)(2,1)S(1)}, u32[]{:S(2)}) copy-start(bf16[4,512,128]{2,1,0:T(8,128)(2,1)S(1)} %collective-permute-done.2.refs_3_) | copy-start | bytes 1572868
  39.4 15.3 %collective-permute-start.6 = (bf16[4,512,128]{2,1,0:T(8,128)(2,1)S(1)}, bf16[4,512,128]{2,1,0:T(8,128)(2,1)}, u32[]{:S(2)}, u32[]{:S(2)}) collective-permute-start(bf16[4,512,128]{2,1,0:T(8,128)(2,1)S(1)} %collective-permute-done.2.refs_3_), channel_id=1, source_target_pairs={{0,8},{8,0},{1,9},{9,1},{2,10},{10,2},{3,11},{11,3},{4,12},{12,4},... | collective-permute-start | bytes 1572872 | tf_op jit(solution)/shard_map/ppermute | solution.py:33
  44.4 10.4 %copy-start.3 = (bf16[4,512,128]{2,1,0:T(8,128)(2,1)}, bf16[4,512,128]{2,1,0:T(8,128)(2,1)S(1)}, u32[]{:S(2)}) copy-start(bf16[4,512,128]{2,1,0:T(8,128)(2,1)S(1)} %collective-permute-done.3.refs_4_) | copy-start | bytes 1572868
  64.8 13.8 %all-to-all-start.1 = ((f32[8,8,4,512]{3,2,1,0:T(4,128)}), f32[8,8,4,512]{3,2,1,0:T(4,128)S(1)}, u32[]{:S(2)}, u32[]{:S(2)}) async-start(f32[8,8,4,512]{3,2,1,0:T(4,128)} %get-tuple-element.16), calls=%async_computation.1 | async-start | bytes 1048576 | tf_op jit(solution)/shard_map/all_to_all | solution.py:293
  97.0 7.3 %collective-permute-start.7 = (bf16[4,1024,128]{2,1,0:T(8,128)(2,1)}, bf16[4,1024,128]{2,1,0:T(8,128)(2,1)S(1)}, u32[]{:S(2)}, u32[]{:S(2)}) collective-permute-start(bf16[4,1024,128]{2,1,0:T(8,128)(2,1)} %get-tuple-element.18), channel_id=1, source_target_pairs={{0,8},{8,0},{1,9},{9,1},{2,10},{10,2},{3,11},{11,3},{4,12},{12,4},... | collective-permute-start | bytes 3145736 | tf_op jit(solution)/shard_map/ppermute | solution.py:33
  98.9 28.6 %all-to-all-start.2 = ((bf16[64,8,256]{2,1,0:T(8,128)(2,1)}), bf16[64,8,256]{2,1,0:T(8,128)(2,1)S(1)}, u32[]{:S(2)}, u32[]{:S(2)}) async-start(bf16[64,8,256]{2,1,0:T(8,128)(2,1)} %bitcast.18), calls=%async_computation.2 | async-start | bytes 524288 | tf_op jit(solution)/shard_map/all_to_all | solution.py:296
  105.9 22.4 %collective-permute-start.10 = (bf16[1024,128]{1,0:T(8,128)(2,1)S(1)}, bf16[1024,128]{1,0:T(8,128)(2,1)S(1)}, u32[]{:S(2)}, u32[]{:S(2)}) collective-permute-start(bf16[1024,128]{1,0:T(8,128)(2,1)S(1)} %get-tuple-element.27), channel_id=1, source_target_pairs={{0,16},{16,32},{32,48},{48,0},{1,17},{17,33},{33,49},{49,1},{2,18}... | collective-permute-start | bytes 786440 | tf_op jit(solution)/shard_map/ppermute | solution.py:33
  108.4 19.9 %collective-permute-start.8 = (bf16[1024,128]{1,0:T(8,128)(2,1)S(1)}, bf16[1024,128]{1,0:T(8,128)(2,1)S(1)}, u32[]{:S(2)}, u32[]{:S(2)}) collective-permute-start(bf16[1024,128]{1,0:T(8,128)(2,1)S(1)} %get-tuple-element.26), channel_id=1, source_target_pairs={{0,48},{16,0},{32,16},{48,32},{1,49},{17,1},{33,17},{49,33},{2,50}... | collective-permute-start | bytes 786440 | tf_op jit(solution)/shard_map/ppermute | solution.py:33
  112.9 15.3 %collective-permute-start.9 = (bf16[1024,128]{1,0:T(8,128)(2,1)S(1)}, bf16[1024,128]{1,0:T(8,128)(2,1)S(1)}, u32[]{:S(2)}, u32[]{:S(2)}) collective-permute-start(bf16[1024,128]{1,0:T(8,128)(2,1)S(1)} %get-tuple-element.28), channel_id=1, source_target_pairs={{0,32},{16,48},{32,0},{48,16},{1,33},{17,49},{33,1},{49,17},{2,34}... | collective-permute-start | bytes 786440 | tf_op jit(solution)/shard_map/ppermute | solution.py:33

commit v4 on v3

--- a/solution.py
+++ b/solution.py
@@ -19,6 +19,7 @@
 TOKENS = 64
 ROWS = 512
 KEYS = ZL * TOKENS
+SHORT_KEYS = 6 * TOKENS
 MASKED = -1e30
 SCALING = 1.0 / math.sqrt(HD)
 LOG2E = math.log2(math.e)
@@ -50,7 +51,7 @@
 
 def prompt_scores(block, kind, info, keys, queries):
     scores = lax.dot_general(keys, queries, NT, preferred_element_type=F32) * SCALE2
-    key = lax.broadcasted_iota(jnp.int32, (KEYS, 1), 0)
+    key = lax.broadcasted_iota(jnp.int32, (keys.shape[0], 1), 0)
     key_pos = (key // TOKENS) * (BLOCKS * TOKENS) + key % TOKENS + (info[0] * CORES + info[1]) * TOKENS
     if kind == 1:
         limit = jnp.zeros((1, ROWS), jnp.int32) + (info[3] - 1)
@@ -65,6 +66,15 @@
     return jnp.where(key_pos <= first_tokens(block, 1, info)[0] + row_tokens(), scores, MASKED)
 
 
+def per_extent(info):
+    def run(body):
+        short = info[3] <= SHORT_KEYS * BLOCKS
+        pl.when(short)(lambda: body(SHORT_KEYS))
+        pl.when(jnp.logical_not(short))(lambda: body(KEYS))
+
+    return run
+
+
 def partial_stats(scores, weight_grad):
     top = jnp.max(scores, axis=0, keepdims=True)
     weights = jnp.exp2(scores - top)
@@ -112,11 +122,13 @@
             stats_s[at, 2 * kind : 2 * kind + 1, :] = stats[0]
             stats_s[at, 2 * kind + 1 : 2 * kind + 2, :] = stats[1]
 
-        for kind in (0, 1):
-            queries, grads = rows_s[block, kind], rows_s[block, 2 + kind]
-            scores = prompt_scores(block, kind, info, kv_ref[:, :HD], queries)
-            weight_grad = lax.dot_general(kv_ref[:, HD:], grads, NT, preferred_element_type=F32)
-            put(kind, partial_stats(scores, weight_grad))
+        @per_extent(info)
+        def _(extent):
+            for kind in (0, 1):
+                queries, grads = rows_s[block, kind], rows_s[block, 2 + kind]
+                scores = prompt_scores(block, kind, info, kv_ref[:extent, :HD], queries)
+                weight_grad = lax.dot_general(kv_ref[:extent, HD:], grads, NT, preferred_element_type=F32)
+                put(kind, partial_stats(scores, weight_grad))
 
         @pl.when(sees_roll(block, info))
         def _():
@@ -161,17 +173,20 @@
     @pl.loop(0, BLOCKS)
     def _(block):
         arrive(block, rows, rows_s, sems)
-        for kind in (0, 1):
-            log_total, delta = combined(stats_ref, block, kind, info)
-            queries, grads = rows_s[block, kind], rows_s[block, 2 + kind]
-            scores = prompt_scores(block, kind, info, kv_ref[:, :HD], queries)
-            weight_grad = lax.dot_general(kv_ref[:, HD:], grads, NT, preferred_element_type=F32)
-            query_t, key_part, value_part = block_grads(
-                scores, weight_grad, log_total, delta, queries, grads, kt_ref[...]
-            )
-            dqt_s[kind] = query_t
-            acc[:, :HD] += key_part
-            acc[:, HD:] += value_part
+
+        @per_extent(info)
+        def _(extent):
+            for kind in (0, 1):
+                log_total, delta = combined(stats_ref, block, kind, info)
+                queries, grads = rows_s[block, kind], rows_s[block, 2 + kind]
+                scores = prompt_scores(block, kind, info, kv_ref[:extent, :HD], queries)
+                weight_grad = lax.dot_general(kv_ref[:extent, HD:], grads, NT, preferred_element_type=F32)
+                query_t, key_part, value_part = block_grads(
+                    scores, weight_grad, log_total, delta, queries, grads, kt_ref[:, :extent]
+                )
+                dqt_s[kind] = query_t
+                acc[:extent, :HD] += key_part
+                acc[:extent, HD:] += value_part
 
         @pl.when(sees_roll(block, info))
         def _():
@@ -296,7 +311,6 @@
     back = lax.all_to_all(
         dkv.reshape(ZL * groups, TOKENS // groups, 2 * HD), FAR, split_axis=0, concat_axis=0, tiled=True
     )
-    dk_prompt, dv_prompt = call_finish(back.reshape(ZL, groups, TOKENS // groups, 2 * HD))
     arrived = shifted(dq_other, "core", 1)
     halves = (dq_same.astype(F32) + arrived.astype(F32)).astype(BF16)
     parts = [halves[0]] + [shifted(halves[steps], "x", -steps) for steps in range(1, X)]
@@ -304,6 +318,8 @@
         sum(part[first : first + ROWS].astype(F32) for part in parts).astype(BF16).reshape(q_prompt.shape)
         for first in (0, ROWS)
     ]
+    back, *dq = lax.optimization_barrier((back, *dq))
+    dk_prompt, dv_prompt = call_finish(back.reshape(ZL, groups, TOKENS // groups, 2 * HD))
     return (dq[0], dk_prompt, dv_prompt, dq[1], drk.reshape(k_roll.shape), drv.reshape(v_roll.shape))
 
 

time: 130 us -> 130 us (level)
    all_to_all x1, waiting for transfers between devices: 12.6 us -> 2.7 us  [per_device(): lax.all_to_all(dkv.reshape(ZL * groups, TOKENS // groups, 2 * HD), FAR, s...]
    ppermute x11, waiting for transfers between devices: 0.03 us -> 9.11 us  [shifted(): lax.ppermute(value, axis, [(i, (i + steps) % count) for i in range(count)])]
  transfers between devices with their start and end apart: 14 -> 14, of which waited for: 3 -> 5; matrix products, arithmetic and copies ran while one was open for 4% -> 5% of each run, Pallas kernels for 1% -> 0%
where the time goes in v4:
time: 130 us; the launch traced here: 129 us
  starting transfers between devices  58.2 us (45%)
  waiting for transfers between devices  32.3 us (25%)
  Pallas kernels  29.7 us (23%)
  other arithmetic  4.27 us (3%)
  local copies, waits for them, and re-layouts  2.77 us (2%)
  between operations  1.57 us (1%)
    ppermute x11, starting transfers between devices, shifted(): lax.ppermute(value, axis, [(i, (i + steps) % count) for i in range(count)])  30.9 us
    pallas_call x1, Pallas kernels, call_grads(): pl.pallas_call(grads_kernel, out_shape=(half, half, jax.ShapeDtypeStruct(...  18.7 us
    all_to_all x1, starting transfers between devices, per_device(): lax.all_to_all(sent, FAR, split_axis=0, concat_axis=0, tiled=True)  18.4 us
    all_to_all x1, waiting for transfers between devices, per_device(): lax.all_to_all(sent, FAR, split_axis=0, concat_axis=0, tiled=True)  10.4 us
    pallas_call x1, Pallas kernels, call_stats(): pl.pallas_call(stats_kernel, out_shape=(jax.ShapeDtypeStruct((BLOCKS, BLO...  10.3 us
    all_to_all x1, waiting for transfers between devices, per_device(): stats = lax.all_to_all(stats, NEAR, split_axis=0, concat_axis=0, tiled=True)  10.1 us
    ppermute x11, waiting for transfers between devices, shifted(): lax.ppermute(value, axis, [(i, (i + steps) % count) for i in range(count)])  9.11 us
    all_to_all x1, starting transfers between devices, per_device(): lax.all_to_all(dkv.reshape(ZL * groups, TOKENS // groups, 2 * HD), FAR, s...  5.38 us
  transfers between devices with their start and end apart: 14, of which 5 were waited for; matrix products, arithmetic and copies ran while one was open for 5% of the time, Pallas kernels for 0%

profile of v4, /device:TPU:32, one launch (start us, length us, event | category | flops | bytes accessed | tf_op | source)
XLA Modules:
  0.0 128.8 jit_solution(15963150650901447569)
XLA Ops:
  0.6 1.2 pad_maximum_fusion.refs_0_
  1.8 3.4 %collective-permute-start = (bf16[4,512,128]{2,1,0:T(8,128)(2,1)S(1)}, bf16[4,512,128]{2,1,0:T(8,128)(2,1)S(1)}, u32[]{:S(2)}, u32[]{:S(2)}) collective-permute-start(bf16[4,512,128]{2,1,0:T(8,128)(2,1)S(1)} %pad_maximum_fusion.refs_0_), channel_id=1, source_target_pairs={{0,16},{16,32},{32,48},{48,0},{1,17},{17,33},{33,49},{49,1},{2,18}... | collective-permute-start | bytes 1572872 | tf_op jit(solution)/shard_map/ppermute | solution.py:34
  5.2 4.6 %collective-permute-start.1 = (bf16[4,512,128]{2,1,0:T(8,128)(2,1)S(1)}, bf16[4,512,128]{2,1,0:T(8,128)(2,1)S(1)}, u32[]{:S(2)}, u32[]{:S(2)}) collective-permute-start(bf16[4,512,128]{2,1,0:T(8,128)(2,1)S(1)} %pad_maximum_fusion.refs_0_), channel_id=1, source_target_pairs={{0,32},{16,48},{32,0},{48,16},{1,33},{17,49},{33,1},{49,17},{2,34}... | collective-permute-start | bytes 1572872 | tf_op jit(solution)/shard_map/ppermute | solution.py:34
  9.9 3.3 %collective-permute-start.2 = (bf16[4,512,128]{2,1,0:T(8,128)(2,1)S(1)}, bf16[4,512,128]{2,1,0:T(8,128)(2,1)S(1)}, u32[]{:S(2)}, u32[]{:S(2)}) collective-permute-start(bf16[4,512,128]{2,1,0:T(8,128)(2,1)S(1)} %pad_maximum_fusion.refs_0_), channel_id=1, source_target_pairs={{0,48},{16,0},{32,16},{48,32},{1,49},{17,1},{33,17},{49,33},{2,50}... | collective-permute-start | bytes 1572872 | tf_op jit(solution)/shard_map/ppermute | solution.py:34
  13.2 0.7 maximum_bitcast_fusion.1
  14.0 0.7 broadcast_in_dim.2
  14.7 18.4 %all-to-all-start = ((bf16[64,8,256]{2,1,0:T(8,128)(2,1)}), bf16[64,8,256]{2,1,0:T(8,128)(2,1)S(1)}, u32[]{:S(2)}, u32[]{:S(2)}) async-start(bf16[64,8,256]{2,1,0:T(8,128)(2,1)} %bitcast.8), calls=%async_computation | async-start | bytes 524288 | tf_op jit(solution)/shard_map/all_to_all | solution.py:301
  33.1 1.9 %collective-permute-start.3 = (bf16[4,512,128]{2,1,0:T(8,128)(2,1)S(1)}, bf16[4,512,128]{2,1,0:T(8,128)(2,1)S(1)}, u32[]{:S(2)}, u32[]{:S(2)}) collective-permute-start(bf16[4,512,128]{2,1,0:T(8,128)(2,1)S(1)} %pad_maximum_fusion.refs_0_), channel_id=1, source_target_pairs={{0,8},{8,0},{1,9},{9,1},{2,10},{10,2},{3,11},{11,3},{4,12},{12,4},... | collective-permute-start | bytes 1572872 | tf_op jit(solution)/shard_map/ppermute | solution.py:34
  35.0 2.4 %collective-permute-start.4 = (bf16[4,512,128]{2,1,0:T(8,128)(2,1)S(1)}, bf16[4,512,128]{2,1,0:T(8,128)(2,1)}, u32[]{:S(2)}, u32[]{:S(2)}) collective-permute-start(bf16[4,512,128]{2,1,0:T(8,128)(2,1)S(1)} %collective-permute-done.refs_1_), channel_id=1, source_target_pairs={{0,8},{8,0},{1,9},{9,1},{2,10},{10,2},{3,11},{11,3},{4,12},{12,4},... | collective-permute-start | bytes 1572872 | tf_op jit(solution)/shard_map/ppermute | solution.py:34
  37.5 1.9 %collective-permute-start.5 = (bf16[4,512,128]{2,1,0:T(8,128)(2,1)S(1)}, bf16[4,512,128]{2,1,0:T(8,128)(2,1)}, u32[]{:S(2)}, u32[]{:S(2)}) collective-permute-start(bf16[4,512,128]{2,1,0:T(8,128)(2,1)S(1)} %collective-permute-done.1.refs_2_), channel_id=1, source_target_pairs={{0,8},{8,0},{1,9},{9,1},{2,10},{10,2},{3,11},{11,3},{4,12},{12,4},... | collective-permute-start | bytes 1572872 | tf_op jit(solution)/shard_map/ppermute | solution.py:34
  39.4 2.4 %collective-permute-start.6 = (bf16[4,512,128]{2,1,0:T(8,128)(2,1)S(1)}, bf16[4,512,128]{2,1,0:T(8,128)(2,1)}, u32[]{:S(2)}, u32[]{:S(2)}) collective-permute-start(bf16[4,512,128]{2,1,0:T(8,128)(2,1)S(1)} %collective-permute-done.2.refs_3_), channel_id=1, source_target_pairs={{0,8},{8,0},{1,9},{9,1},{2,10},{10,2},{3,11},{11,3},{4,12},{12,4},... | collective-permute-start | bytes 1572872 | tf_op jit(solution)/shard_map/ppermute | solution.py:34
  42.5 0.8 copy.24
  43.3 0.8 copy.25
  44.2 0.1 copy.26.refs_9_.rkv_ref
  44.3 0.1 concatenate.10.info
  44.4 10.4 %all-to-all-done = bf16[64,8,256]{2,1,0:T(8,128)(2,1)S(1)} async-done(((bf16[64,8,256]{2,1,0:T(8,128)(2,1)}), bf16[64,8,256]{2,1,0:T(8,128)(2,1)S(1)}, u32[]{:S(2)}, u32[]{:S(2)}) %all-to-all-start) | async-done | bytes 262176 | tf_op jit(solution)/shard_map/all_to_all | solution.py:301
  54.8 10.3 %row_stats.1 = (f32[8,8,4,512]{3,2,1,0:T(4,128)}, bf16[8,4,512,128]{3,2,1,0:T(8,128)(2,1)}) custom-call(s32[20]{0:T(128)S(1)} %concatenate.10.info, bf16[4,512,128]{2,1,0:T(8,128)(2,1)S(1)} %pad_maximum_fusion.refs_0_, bf16[4,512,128]{2,1,0:T(8,128)(2,1)S(1)} %collective-permute-done.refs_1_, bf16[4,512,128]{2,1,0:T(8,128)(2,1)} %copy-done.1, ...), custom_call_target="tpu_custom_call" | custom-call | flops 2415919104 | bytes 5242880 | tf_op jit(solution)/shard_map/row_stats/pallas_call | solution.py:242
  65.0 3.5 %all-to-all-start.1 = ((f32[8,8,4,512]{3,2,1,0:T(4,128)}), f32[8,8,4,512]{3,2,1,0:T(4,128)S(1)}, u32[]{:S(2)}, u32[]{:S(2)}) async-start(f32[8,8,4,512]{3,2,1,0:T(4,128)} %get-tuple-element.19), calls=%async_computation.1 | async-start | bytes 1048576 | tf_op jit(solution)/shard_map/all_to_all | solution.py:308
  68.6 0.1 copy.29
  68.7 10.1 %all-to-all-done.1.stats_ref = f32[8,8,4,512]{3,2,1,0:T(4,128)S(1)} async-done(((f32[8,8,4,512]{3,2,1,0:T(4,128)}), f32[8,8,4,512]{3,2,1,0:T(4,128)S(1)}, u32[]{:S(2)}, u32[]{:S(2)}) %all-to-all-start.1) | async-done | bytes 524320 | tf_op jit(solution)/shard_map/all_to_all | solution.py:308
  78.8 18.7 %row_grads.1 = (bf16[4,1024,128]{2,1,0:T(8,128)(2,1)}, bf16[4,1024,128]{2,1,0:T(8,128)(2,1)}, bf16[512,256]{1,0:T(8,128)(2,1)}, bf16[64,128]{1,0:T(8,128)(2,1)}, bf16[64,128]{1,0:T(8,128)(2,1)}) custom-call(s32[20]{0:T(128)S(1)} %concatenate.10.info, bf16[8,4,512,128]{3,2,1,0:T(8,128)(2,1)} %get-tuple-element.18.rows_ref, ...), custom_call_target="tpu_custom_call" | custom-call | flops 6039797760 | bytes 7340032 | tf_op jit(solution)/shard_map/row_grads/pallas_call | solution.py:265
  97.6 1.9 %collective-permute-start.7 = (bf16[4,1024,128]{2,1,0:T(8,128)(2,1)}, bf16[4,1024,128]{2,1,0:T(8,128)(2,1)S(1)}, u32[]{:S(2)}, u32[]{:S(2)}) collective-permute-start(bf16[4,1024,128]{2,1,0:T(8,128)(2,1)} %get-tuple-element.22), channel_id=1, source_target_pairs={{0,8},{8,0},{1,9},{9,1},{2,10},{10,2},{3,11},{11,3},{4,12},{12,4},... | collective-permute-start | bytes 3145736 | tf_op jit(solution)/shard_map/ppermute | solution.py:34
  99.5 5.4 %all-to-all-start.2 = ((bf16[64,8,256]{2,1,0:T(8,128)(2,1)}), bf16[64,8,256]{2,1,0:T(8,128)(2,1)S(1)}, u32[]{:S(2)}, u32[]{:S(2)}) async-start(bf16[64,8,256]{2,1,0:T(8,128)(2,1)} %bitcast.13), calls=%async_computation.2 | async-start | bytes 524288 | tf_op jit(solution)/shard_map/all_to_all | solution.py:311
  104.9 1.5 %add_convert_fusion = bf16[4,1024,128]{2,1,0:T(8,128)(2,1)S(1)} fusion(bf16[4,1024,128]{2,1,0:T(8,128)(2,1)S(1)} %collective-permute-done.7, bf16[4,1024,128]{2,1,0:T(8,128)(2,1)} %get-tuple-element.21), kind=kLoop, calls=%fused_computation | loop fusion | flops 2097152 | bytes 3145728 | tf_op jit(solution)/shard_map/convert_element_type | solution.py:315
  106.5 2.5 %collective-permute-start.10 = (bf16[1024,128]{1,0:T(8,128)(2,1)S(1)}, bf16[1024,128]{1,0:T(8,128)(2,1)S(1)}, u32[]{:S(2)}, u32[]{:S(2)}) collective-permute-start(bf16[1024,128]{1,0:T(8,128)(2,1)S(1)} %get-tuple-element.33), channel_id=1, source_target_pairs={{0,16},{16,32},{32,48},{48,0},{1,17},{17,33},{33,49},{49,1},{2,18}... | collective-permute-start | bytes 786440 | tf_op jit(solution)/shard_map/ppermute | solution.py:34
  109.0 4.6 %collective-permute-start.8 = (bf16[1024,128]{1,0:T(8,128)(2,1)S(1)}, bf16[1024,128]{1,0:T(8,128)(2,1)S(1)}, u32[]{:S(2)}, u32[]{:S(2)}) collective-permute-start(bf16[1024,128]{1,0:T(8,128)(2,1)S(1)} %get-tuple-element.32), channel_id=1, source_target_pairs={{0,48},{16,0},{32,16},{48,32},{1,49},{17,1},{33,17},{49,33},{2,50}... | collective-permute-start | bytes 786440 | tf_op jit(solution)/shard_map/ppermute | solution.py:34
  113.5 1.9 %collective-permute-start.9 = (bf16[1024,128]{1,0:T(8,128)(2,1)S(1)}, bf16[1024,128]{1,0:T(8,128)(2,1)S(1)}, u32[]{:S(2)}, u32[]{:S(2)}) collective-permute-start(bf16[1024,128]{1,0:T(8,128)(2,1)S(1)} %get-tuple-element.34), channel_id=1, source_target_pairs={{0,32},{16,48},{32,0},{48,16},{1,33},{17,49},{33,1},{49,17},{2,34}... | collective-permute-start | bytes 786440 | tf_op jit(solution)/shard_map/ppermute | solution.py:34
  115.5 2.3 %collective-permute-done.10 = bf16[1024,128]{1,0:T(8,128)(2,1)S(1)} collective-permute-done((bf16[1024,128]{1,0:T(8,128)(2,1)S(1)}, bf16[1024,128]{1,0:T(8,128)(2,1)S(1)}, u32[]{:S(2)}, u32[]{:S(2)}) %collective-permute-start.10) | collective-permute-done | bytes 262176 | tf_op jit(solution)/shard_map/ppermute | solution.py:34
  117.7 6.8 %collective-permute-done.8 = bf16[1024,128]{1,0:T(8,128)(2,1)S(1)} collective-permute-done((bf16[1024,128]{1,0:T(8,128)(2,1)S(1)}, bf16[1024,128]{1,0:T(8,128)(2,1)S(1)}, u32[]{:S(2)}, u32[]{:S(2)}) %collective-permute-start.8) | collective-permute-done | bytes 262176 | tf_op jit(solution)/shard_map/ppermute | solution.py:34
  124.6 0.8 fusion.7
  125.4 2.7 %all-to-all-done.2 = bf16[64,8,256]{2,1,0:T(8,128)(2,1)S(1)} async-done(((bf16[64,8,256]{2,1,0:T(8,128)(2,1)}), bf16[64,8,256]{2,1,0:T(8,128)(2,1)S(1)}, u32[]{:S(2)}, u32[]{:S(2)}) %all-to-all-start.2) | async-done | bytes 262176 | tf_op jit(solution)/shard_map/all_to_all | solution.py:311
  128.1 0.7 sum_planes.1
  (22 shorter events, 0.1 us)
Async XLA Ops:
  0.6 43.6 %copy-start = (s32[16]{0:T(128)S(1)}, s32[16]{0:T(128)}, u32[]{:S(2)}) copy-start(s32[16]{0:T(128)} %param.19) | copy-start | bytes 196
  1.8 33.2 %collective-permute-start = (bf16[4,512,128]{2,1,0:T(8,128)(2,1)S(1)}, bf16[4,512,128]{2,1,0:T(8,128)(2,1)S(1)}, u32[]{:S(2)}, u32[]{:S(2)}) collective-permute-start(bf16[4,512,128]{2,1,0:T(8,128)(2,1)S(1)} %pad_maximum_fusion.refs_0_), channel_id=1, source_target_pairs={{0,16},{16,32},{32,48},{48,0},{1,17},{17,33},{33,49},{49,1},{2,18}... | collective-permute-start | bytes 1572872 | tf_op jit(solution)/shard_map/ppermute | solution.py:34
  5.2 32.2 %collective-permute-start.1 = (bf16[4,512,128]{2,1,0:T(8,128)(2,1)S(1)}, bf16[4,512,128]{2,1,0:T(8,128)(2,1)S(1)}, u32[]{:S(2)}, u32[]{:S(2)}) collective-permute-start(bf16[4,512,128]{2,1,0:T(8,128)(2,1)S(1)} %pad_maximum_fusion.refs_0_), channel_id=1, source_target_pairs={{0,32},{16,48},{32,0},{48,16},{1,33},{17,49},{33,1},{49,17},{2,34}... | collective-permute-start | bytes 1572872 | tf_op jit(solution)/shard_map/ppermute | solution.py:34
  9.9 29.5 %collective-permute-start.2 = (bf16[4,512,128]{2,1,0:T(8,128)(2,1)S(1)}, bf16[4,512,128]{2,1,0:T(8,128)(2,1)S(1)}, u32[]{:S(2)}, u32[]{:S(2)}) collective-permute-start(bf16[4,512,128]{2,1,0:T(8,128)(2,1)S(1)} %pad_maximum_fusion.refs_0_), channel_id=1, source_target_pairs={{0,48},{16,0},{32,16},{48,32},{1,49},{17,1},{33,17},{49,33},{2,50}... | collective-permute-start | bytes 1572872 | tf_op jit(solution)/shard_map/ppermute | solution.py:34
  14.7 40.0 %all-to-all-start = ((bf16[64,8,256]{2,1,0:T(8,128)(2,1)}), bf16[64,8,256]{2,1,0:T(8,128)(2,1)S(1)}, u32[]{:S(2)}, u32[]{:S(2)}) async-start(bf16[64,8,256]{2,1,0:T(8,128)(2,1)} %bitcast.8), calls=%async_computation | async-start | bytes 524288 | tf_op jit(solution)/shard_map/all_to_all | solution.py:301
  33.1 11.3 %collective-permute-start.3 = (bf16[4,512,128]{2,1,0:T(8,128)(2,1)S(1)}, bf16[4,512,128]{2,1,0:T(8,128)(2,1)S(1)}, u32[]{:S(2)}, u32[]{:S(2)}) collective-permute-start(bf16[4,512,128]{2,1,0:T(8,128)(2,1)S(1)} %pad_maximum_fusion.refs_0_), channel_id=1, source_target_pairs={{0,8},{8,0},{1,9},{9,1},{2,10},{10,2},{3,11},{11,3},{4,12},{12,4},... | collective-permute-start | bytes 1572872 | tf_op jit(solution)/shard_map/ppermute | solution.py:34
  35.0 19.7 %collective-permute-start.4 = (bf16[4,512,128]{2,1,0:T(8,128)(2,1)S(1)}, bf16[4,512,128]{2,1,0:T(8,128)(2,1)}, u32[]{:S(2)}, u32[]{:S(2)}) collective-permute-start(bf16[4,512,128]{2,1,0:T(8,128)(2,1)S(1)} %collective-permute-done.refs_1_), channel_id=1, source_target_pairs={{0,8},{8,0},{1,9},{9,1},{2,10},{10,2},{3,11},{11,3},{4,12},{12,4},... | collective-permute-start | bytes 1572872 | tf_op jit(solution)/shard_map/ppermute | solution.py:34
  37.5 17.3 %copy-start.1 = (bf16[4,512,128]{2,1,0:T(8,128)(2,1)}, bf16[4,512,128]{2,1,0:T(8,128)(2,1)S(1)}, u32[]{:S(2)}) copy-start(bf16[4,512,128]{2,1,0:T(8,128)(2,1)S(1)} %collective-permute-done.1.refs_2_) | copy-start | bytes 1572868
  37.5 17.3 %collective-permute-start.5 = (bf16[4,512,128]{2,1,0:T(8,128)(2,1)S(1)}, bf16[4,512,128]{2,1,0:T(8,128)(2,1)}, u32[]{:S(2)}, u32[]{:S(2)}) collective-permute-start(bf16[4,512,128]{2,1,0:T(8,128)(2,1)S(1)} %collective-permute-done.1.refs_2_), channel_id=1, source_target_pairs={{0,8},{8,0},{1,9},{9,1},{2,10},{10,2},{3,11},{11,3},{4,12},{12,4},... | collective-permute-start | bytes 1572872 | tf_op jit(solution)/shard_map/ppermute | solution.py:34
  39.4 15.4 %copy-start.2 = (bf16[4,512,128]{2,1,0:T(8,128)(2,1)}, bf16[4,512,128]{2,1,0:T(8,128)(2,1)S(1)}, u32[]{:S(2)}) copy-start(bf16[4,512,128]{2,1,0:T(8,128)(2,1)S(1)} %collective-permute-done.2.refs_3_) | copy-start | bytes 1572868
  39.4 15.3 %collective-permute-start.6 = (bf16[4,512,128]{2,1,0:T(8,128)(2,1)S(1)}, bf16[4,512,128]{2,1,0:T(8,128)(2,1)}, u32[]{:S(2)}, u32[]{:S(2)}) collective-permute-start(bf16[4,512,128]{2,1,0:T(8,128)(2,1)S(1)} %collective-permute-done.2.refs_3_), channel_id=1, source_target_pairs={{0,8},{8,0},{1,9},{9,1},{2,10},{10,2},{3,11},{11,3},{4,12},{12,4},... | collective-permute-start | bytes 1572872 | tf_op jit(solution)/shard_map/ppermute | solution.py:34
  44.4 10.4 %copy-start.3 = (bf16[4,512,128]{2,1,0:T(8,128)(2,1)}, bf16[4,512,128]{2,1,0:T(8,128)(2,1)S(1)}, u32[]{:S(2)}) copy-start(bf16[4,512,128]{2,1,0:T(8,128)(2,1)S(1)} %collective-permute-done.3.refs_4_) | copy-start | bytes 1572868
  65.0 13.8 %all-to-all-start.1 = ((f32[8,8,4,512]{3,2,1,0:T(4,128)}), f32[8,8,4,512]{3,2,1,0:T(4,128)S(1)}, u32[]{:S(2)}, u32[]{:S(2)}) async-start(f32[8,8,4,512]{3,2,1,0:T(4,128)} %get-tuple-element.19), calls=%async_computation.1 | async-start | bytes 1048576 | tf_op jit(solution)/shard_map/all_to_all | solution.py:308
  97.6 7.3 %collective-permute-start.7 = (bf16[4,1024,128]{2,1,0:T(8,128)(2,1)}, bf16[4,1024,128]{2,1,0:T(8,128)(2,1)S(1)}, u32[]{:S(2)}, u32[]{:S(2)}) collective-permute-start(bf16[4,1024,128]{2,1,0:T(8,128)(2,1)} %get-tuple-element.22), channel_id=1, source_target_pairs={{0,8},{8,0},{1,9},{9,1},{2,10},{10,2},{3,11},{11,3},{4,12},{12,4},... | collective-permute-start | bytes 3145736 | tf_op jit(solution)/shard_map/ppermute | solution.py:34
  99.5 28.6 %all-to-all-start.2 = ((bf16[64,8,256]{2,1,0:T(8,128)(2,1)}), bf16[64,8,256]{2,1,0:T(8,128)(2,1)S(1)}, u32[]{:S(2)}, u32[]{:S(2)}) async-start(bf16[64,8,256]{2,1,0:T(8,128)(2,1)} %bitcast.13), calls=%async_computation.2 | async-start | bytes 524288 | tf_op jit(solution)/shard_map/all_to_all | solution.py:311
  106.5 11.3 %collective-permute-start.10 = (bf16[1024,128]{1,0:T(8,128)(2,1)S(1)}, bf16[1024,128]{1,0:T(8,128)(2,1)S(1)}, u32[]{:S(2)}, u32[]{:S(2)}) collective-permute-start(bf16[1024,128]{1,0:T(8,128)(2,1)S(1)} %get-tuple-element.33), channel_id=1, source_target_pairs={{0,16},{16,32},{32,48},{48,0},{1,17},{17,33},{33,49},{49,1},{2,18}... | collective-permute-start | bytes 786440 | tf_op jit(solution)/shard_map/ppermute | solution.py:34
  109.0 15.6 %collective-permute-start.8 = (bf16[1024,128]{1,0:T(8,128)(2,1)S(1)}, bf16[1024,128]{1,0:T(8,128)(2,1)S(1)}, u32[]{:S(2)}, u32[]{:S(2)}) collective-permute-start(bf16[1024,128]{1,0:T(8,128)(2,1)S(1)} %get-tuple-element.32), channel_id=1, source_target_pairs={{0,48},{16,0},{32,16},{48,32},{1,49},{17,1},{33,17},{49,33},{2,50}... | collective-permute-start | bytes 786440 | tf_op jit(solution)/shard_map/ppermute | solution.py:34
  113.5 11.0 %collective-permute-start.9 = (bf16[1024,128]{1,0:T(8,128)(2,1)S(1)}, bf16[1024,128]{1,0:T(8,128)(2,1)S(1)}, u32[]{:S(2)}, u32[]{:S(2)}) collective-permute-start(bf16[1024,128]{1,0:T(8,128)(2,1)S(1)} %get-tuple-element.34), channel_id=1, source_target_pairs={{0,32},{16,48},{32,0},{48,16},{1,33},{17,49},{33,1},{49,17},{2,34}... | collective-permute-start | bytes 786440 | tf_op jit(solution)/shard_map/ppermute | solution.py:34
